TPU v7x, 512 devices: a whole 4x4x16 slice. The times are simulated.
512 devices in a mesh: dp: 4 (over z_hi), context: 128 (over z_lo, y, x, core).
Axes of the slice: x: 4, y: 4, z: 16 (z_hi: 4, z_lo: 4; z = z_hi * 4 + z_lo), core: 2. Of those that a mesh axis runs over, the one named last changes fastest.
Arguments:
- input_gate: bfloat16 [4, 16384, 256], P('dp', 'context'), may hold values from -6 to 6
- values: bfloat16 [4, 16384, 256], P('dp', 'context'), may hold values from -6 to 6
- output_gate: bfloat16 [4, 16384, 256], P('dp', 'context'), may hold values from -6 to 6
- grad_out: bfloat16 [4, 16384, 256], P('dp', 'context'), may hold values from -6 to 6
- filter_taps: bfloat16 [256, 16384], P('context'), may hold values from -0.046875 to 0.046875
- skip_gain: float32 [256], replicated, may hold values from -4 to 4
Outputs:
- grad_input_gate: bfloat16 [4, 16384, 256], P('dp', 'context')
- grad_values: bfloat16 [4, 16384, 256], P('dp', 'context')
- grad_output_gate: bfloat16 [4, 16384, 256], P('dp', 'context')
- filter_grad: float32 [256, 16384], P('context', 'dp')
- skip_grad: float32 [256], replicated
All inputs are finite; a program needn't handle non-finite values.
Results may differ from a plain program's by a relative error of at most 0.014.
Values may be sent and summed in bfloat16 or wider, within the bound.
A program may use at most 64 MiB of HBM per device.

v0:
```python
import math

import jax
import jax.numpy as jnp
from jax import lax
from jax.sharding import PartitionSpec as P


def dft_tables(pieces, block_len):
    outer = 2 * pieces
    total = outer * block_len

    def phase(first, second, modulus):
        product = first[:, None] * second[None, :] % modulus
        return product.astype(jnp.float32) * (2.0 * math.pi / modulus)

    across = jnp.arange(pieces, dtype=jnp.int32)
    outer_index = jnp.arange(outer, dtype=jnp.int32)
    inner_index = jnp.arange(block_len, dtype=jnp.int32)
    first_angle = phase(outer_index, across, outer)
    entry = jnp.stack([jnp.cos(first_angle), -jnp.sin(first_angle)]).astype(jnp.bfloat16)
    twist_angle = phase(outer_index, inner_index, total)
    twist_cos = jnp.cos(twist_angle)
    twist_sin = jnp.sin(twist_angle)
    inner_angle = phase(inner_index, inner_index, block_len)
    cosine = jnp.cos(inner_angle)
    sine = jnp.sin(inner_angle)
    forward_inner = jnp.stack([jnp.stack([cosine, -sine], 1), jnp.stack([sine, cosine], 1)]).astype(
        jnp.bfloat16
    )
    inverse_inner = jnp.stack([jnp.stack([cosine, sine], 1), jnp.stack([-sine, cosine], 1)]).astype(
        jnp.bfloat16
    )
    last_angle = phase(across, outer_index, outer)
    leave = jnp.stack([jnp.cos(last_angle), -jnp.sin(last_angle)], 1).astype(jnp.bfloat16)
    return (entry, twist_cos, twist_sin, forward_inner, inverse_inner, leave, 1.0 / total)


def transform(signal, tables):
    entry, twist_cos, twist_sin, forward_inner = (tables[0], tables[1], tables[2], tables[3])
    pieces = entry.shape[2]
    block_len = twist_cos.shape[1]
    shaped = signal.reshape(signal.shape[0], pieces, block_len)
    section = jnp.einsum("pka,rab->prkb", entry, shaped, preferred_element_type=jnp.float32)
    real_part = section[0] * twist_cos + section[1] * twist_sin
    imag_part = section[1] * twist_cos - section[0] * twist_sin
    turned = jnp.stack([real_part, imag_part]).astype(jnp.bfloat16)
    return jnp.einsum("prkb,pbqm->qrkm", turned, forward_inner, preferred_element_type=jnp.float32)


def untransform(spectrum, tables):
    twist_cos, twist_sin, inverse_inner, leave, scale = (
        tables[1],
        tables[2],
        tables[4],
        tables[5],
        tables[6],
    )
    section = jnp.einsum(
        "prkm,pmqb->qrkb", spectrum, inverse_inner, preferred_element_type=jnp.float32
    )
    real_part = section[0] * twist_cos - section[1] * twist_sin
    imag_part = section[1] * twist_cos + section[0] * twist_sin
    turned = jnp.stack([real_part, imag_part]).astype(jnp.bfloat16)
    result = jnp.einsum("apk,prkb->rab", leave, turned, preferred_element_type=jnp.float32)
    return (result * scale).reshape(result.shape[0], -1)


def convolve(mixed_cols, grad_cols, kernel, tables):
    source = transform(mixed_cols, tables)
    incoming = transform(grad_cols, tables)
    forward_conv = jnp.stack(
        [
            source[0] * kernel[0] - source[1] * kernel[1],
            source[0] * kernel[1] + source[1] * kernel[0],
        ]
    ).astype(jnp.bfloat16)
    backward_conv = jnp.stack(
        [
            kernel[0] * incoming[0] + kernel[1] * incoming[1],
            kernel[0] * incoming[1] - kernel[1] * incoming[0],
        ]
    ).astype(jnp.bfloat16)
    kernel_grad = jnp.stack(
        [
            source[0] * incoming[0] + source[1] * incoming[1],
            source[0] * incoming[1] - source[1] * incoming[0],
        ]
    ).astype(jnp.bfloat16)
    conv_out = untransform(forward_conv, tables).astype(jnp.bfloat16)
    conv_back = untransform(backward_conv, tables).astype(jnp.bfloat16)
    filter_term = untransform(kernel_grad, tables)
    return (conv_out, conv_back, filter_term)


def per_device(input_gate, values, output_gate, grad_out, filter_taps, skip_gain):
    pieces = lax.axis_size("context")
    channels = filter_taps.shape[0]
    length = filter_taps.shape[1]
    tables = dft_tables(pieces, length // pieces)
    offset = lax.axis_index("context") * channels
    gate_in = input_gate[0]
    value_rows = values[0]
    gate_out = output_gate[0]
    cotangent = grad_out[0]
    kernel = transform(filter_taps, tables)
    gate_cols, value_cols, out_cols, cot_cols = (
        lax.all_to_all(gate_in.T, "context", split_axis=0, concat_axis=1, tiled=True),
        lax.all_to_all(value_rows.T, "context", split_axis=0, concat_axis=1, tiled=True),
        lax.all_to_all(gate_out.T, "context", split_axis=0, concat_axis=1, tiled=True),
        lax.all_to_all(cotangent.T, "context", split_axis=0, concat_axis=1, tiled=True),
    )
    own_skip = lax.dynamic_slice_in_dim(skip_gain, offset, channels)[:, None]
    mixed = (gate_cols.astype(jnp.float32) * value_cols.astype(jnp.float32)).astype(jnp.bfloat16)
    grad_mix = (cot_cols.astype(jnp.float32) * out_cols.astype(jnp.float32)).astype(jnp.bfloat16)
    conv_out, conv_back, filter_term = convolve(mixed, grad_mix, kernel, tables)
    gated = conv_out.astype(jnp.float32) + own_skip * mixed.astype(jnp.float32)
    grad_out_cols = (cot_cols.astype(jnp.float32) * gated).astype(jnp.bfloat16)
    grad_mixed = conv_back.astype(jnp.float32) + own_skip * grad_mix.astype(jnp.float32)
    grad_in_cols = (grad_mixed * value_cols.astype(jnp.float32)).astype(jnp.bfloat16)
    grad_value_cols = (grad_mixed * gate_cols.astype(jnp.float32)).astype(jnp.bfloat16)
    input_t, value_t, output_t = (
        lax.all_to_all(grad_in_cols, "context", split_axis=1, concat_axis=0, tiled=True),
        lax.all_to_all(grad_value_cols, "context", split_axis=1, concat_axis=0, tiled=True),
        lax.all_to_all(grad_out_cols, "context", split_axis=1, concat_axis=0, tiled=True),
    )
    grad_input = input_t.T
    grad_value = value_t.T
    grad_output = output_t.T
    skip_term = jnp.sum(grad_mix.astype(jnp.float32) * mixed.astype(jnp.float32), axis=1)
    scale = 1.0 / math.sqrt(lax.axis_size("dp") * length)
    filter_grad = (
        lax.psum_scatter(
            filter_term.astype(jnp.bfloat16), "dp", scatter_dimension=1, tiled=True
        ).astype(jnp.float32)
        * scale
    )
    placed = lax.dynamic_update_slice_in_dim(
        jnp.zeros((skip_gain.shape[0],), jnp.float32), skip_term, offset, 0
    )
    skip_grad = lax.psum(placed, ("dp", "context")) * scale
    return (grad_input[None], grad_value[None], grad_output[None], filter_grad, skip_grad)


def solution(mesh):
    return jax.shard_map(
        per_device,
        mesh=mesh,
        in_specs=(
            P("dp", "context", None),
            P("dp", "context", None),
            P("dp", "context", None),
            P("dp", "context", None),
            P("context", None),
            P(),
        ),
        out_specs=(
            P("dp", "context", None),
            P("dp", "context", None),
            P("dp", "context", None),
            P("context", "dp"),
            P(),
        ),
        check_vma=False,
    )
```

profile of v0, /device:TPU:1, one launch (start us, length us, event | category | flops | bytes accessed | tf_op | source)
XLA Modules:
  0.0 337.3 jit_solution(350567711413606809)
XLA Ops:
  7.2 1.6 copy.77
  8.7 13.8 %all-to-all-start.4 = ((bf16[128,2,128]{2,1,0:T(2,128)(2,1)}), bf16[128,2,128]{2,1,0:T(2,128)(2,1)S(1)}, u32[]{:S(2)}, u32[]{:S(2)}) async-start(bf16[128,2,128]{2,1,0:T(2,128)(2,1)} %bitcast.51), calls=%async_computation.4 | async-start | bytes 131072 | tf_op jit(solution)/shard_map/all_to_all | solution.py:108
  22.6 1.6 copy.66
  24.4 8.1 %all-to-all-done.4 = bf16[128,2,128]{2,1,0:T(2,128)(2,1)S(1)} async-done(((bf16[128,2,128]{2,1,0:T(2,128)(2,1)}), bf16[128,2,128]{2,1,0:T(2,128)(2,1)S(1)}, u32[]{:S(2)}, u32[]{:S(2)}) %all-to-all-start.4) | async-done | bytes 65568 | tf_op jit(solution)/shard_map/all_to_all | solution.py:108
  32.5 5.9 %all-to-all-start.1 = ((bf16[128,2,128]{2,1,0:T(2,128)(2,1)}), bf16[128,2,128]{2,1,0:T(2,128)(2,1)S(1)}, u32[]{:S(2)}, u32[]{:S(2)}) async-start(bf16[128,2,128]{2,1,0:T(2,128)(2,1)} %bitcast.22), calls=%async_computation.1 | async-start | bytes 131072 | tf_op jit(solution)/shard_map/all_to_all | solution.py:110
  38.7 1.6 copy.64
  40.8 7.7 %all-to-all-done.1 = bf16[128,2,128]{2,1,0:T(2,128)(2,1)S(1)} async-done(((bf16[128,2,128]{2,1,0:T(2,128)(2,1)}), bf16[128,2,128]{2,1,0:T(2,128)(2,1)S(1)}, u32[]{:S(2)}, u32[]{:S(2)}) %all-to-all-start.1) | async-done | bytes 65568 | tf_op jit(solution)/shard_map/all_to_all | solution.py:110
  48.5 5.9 %all-to-all-start = ((bf16[128,2,128]{2,1,0:T(2,128)(2,1)}), bf16[128,2,128]{2,1,0:T(2,128)(2,1)S(1)}, u32[]{:S(2)}, u32[]{:S(2)}) async-start(bf16[128,2,128]{2,1,0:T(2,128)(2,1)} %bitcast.18), calls=%async_computation | async-start | bytes 131072 | tf_op jit(solution)/shard_map/all_to_all | solution.py:111
  55.0 1.6 copy.74
  56.5 1.0 convolution_bitcast_fusion.8
  57.6 6.9 %all-to-all-done = bf16[128,2,128]{2,1,0:T(2,128)(2,1)S(1)} async-done(((bf16[128,2,128]{2,1,0:T(2,128)(2,1)}), bf16[128,2,128]{2,1,0:T(2,128)(2,1)S(1)}, u32[]{:S(2)}, u32[]{:S(2)}) %all-to-all-start) | async-done | bytes 65568 | tf_op jit(solution)/shard_map/all_to_all | solution.py:111
  64.5 5.9 %all-to-all-start.2 = ((bf16[128,2,128]{2,1,0:T(2,128)(2,1)}), bf16[128,2,128]{2,1,0:T(2,128)(2,1)S(1)}, u32[]{:S(2)}, u32[]{:S(2)}) async-start(bf16[128,2,128]{2,1,0:T(2,128)(2,1)} %bitcast.43), calls=%async_computation.2 | async-start | bytes 131072 | tf_op jit(solution)/shard_map/all_to_all | solution.py:109
  72.3 8.1 %all-to-all-done.2 = bf16[128,2,128]{2,1,0:T(2,128)(2,1)S(1)} async-done(((bf16[128,2,128]{2,1,0:T(2,128)(2,1)}), bf16[128,2,128]{2,1,0:T(2,128)(2,1)S(1)}, u32[]{:S(2)}, u32[]{:S(2)}) %all-to-all-start.2) | async-done | bytes 65568 | tf_op jit(solution)/shard_map/all_to_all | solution.py:109
  83.5 0.8 copy.86
  84.2 5.9 %all-to-all-start.6 = ((bf16[2,128,128]{2,0,1:T(2,128)(2,1)}), bf16[2,128,128]{2,0,1:T(2,128)(2,1)S(1)}, u32[]{:S(2)}, u32[]{:S(2)}) async-start(bf16[2,128,128]{2,0,1:T(2,128)(2,1)} %copy.86), calls=%async_computation.6 | async-start | bytes 131072 | tf_op jit(solution)/shard_map/all_to_all | solution.py:125
  90.4 0.8 copy.79
  91.2 9.0 %all-to-all-done.6 = bf16[2,128,128]{2,0,1:T(2,128)(2,1)S(1)} async-done(((bf16[2,128,128]{2,0,1:T(2,128)(2,1)}), bf16[2,128,128]{2,0,1:T(2,128)(2,1)S(1)}, u32[]{:S(2)}, u32[]{:S(2)}) %all-to-all-start.6) | async-done | bytes 65568 | tf_op jit(solution)/shard_map/all_to_all | solution.py:125
  100.2 5.9 %all-to-all-start.5 = ((bf16[2,128,128]{2,0,1:T(2,128)(2,1)}), bf16[2,128,128]{2,0,1:T(2,128)(2,1)S(1)}, u32[]{:S(2)}, u32[]{:S(2)}) async-start(bf16[2,128,128]{2,0,1:T(2,128)(2,1)} %copy.79), calls=%async_computation.5 | async-start | bytes 131072 | tf_op jit(solution)/shard_map/all_to_all | solution.py:124
  106.4 0.8 copy.76
  107.2 7.4 %copy.132 = bf16[2,128,128]{0,2,1:T(8,128)(2,1)} copy(bf16[2,128,128]{1,2,0:T(8,128)(2,1)S(1)} %fusion.14) | data formatting | bytes 131072
  114.9 194.9 %psum.7 = f32[256]{0:T(256)S(1)} all-reduce(f32[256]{0:T(256)S(1)} %dynamic_update_slice.3), channel_id=1, replica_groups=mesh['dp'=4,'context'=128] {'dp','context'}, use_global_device_ids=true, to_apply=%region_2.3 | all-reduce | flops 256 | bytes 2048 | tf_op jit(solution)/shard_map/psum | solution.py:141
  310.4 1.6 copy.131
  312.0 7.7 %all-to-all-start.3 = ((bf16[2,128,128]{2,0,1:T(2,128)(2,1)}), bf16[2,128,128]{2,0,1:T(2,128)(2,1)S(1)}, u32[]{:S(2)}, u32[]{:S(2)}) async-start(bf16[2,128,128]{2,0,1:T(2,128)(2,1)} %copy.76), calls=%async_computation.3 | async-start | bytes 131072 | tf_op jit(solution)/shard_map/all_to_all | solution.py:123
  321.8 7.8 %all-to-all-done.3 = bf16[2,128,128]{2,0,1:T(2,128)(2,1)S(1)} async-done(((bf16[2,128,128]{2,0,1:T(2,128)(2,1)}), bf16[2,128,128]{2,0,1:T(2,128)(2,1)S(1)}, u32[]{:S(2)}, u32[]{:S(2)}) %all-to-all-start.3) | async-done | bytes 65568 | tf_op jit(solution)/shard_map/all_to_all | solution.py:123
  (37 shorter events, 10.8 us)
Async XLA Ops:
  8.7 23.8 %all-to-all-start.4 = ((bf16[128,2,128]{2,1,0:T(2,128)(2,1)}), bf16[128,2,128]{2,1,0:T(2,128)(2,1)S(1)}, u32[]{:S(2)}, u32[]{:S(2)}) async-start(bf16[128,2,128]{2,1,0:T(2,128)(2,1)} %bitcast.51), calls=%async_computation.4 | async-start | bytes 131072 | tf_op jit(solution)/shard_map/all_to_all | solution.py:108
  32.5 16.0 %all-to-all-start.1 = ((bf16[128,2,128]{2,1,0:T(2,128)(2,1)}), bf16[128,2,128]{2,1,0:T(2,128)(2,1)S(1)}, u32[]{:S(2)}, u32[]{:S(2)}) async-start(bf16[128,2,128]{2,1,0:T(2,128)(2,1)} %bitcast.22), calls=%async_computation.1 | async-start | bytes 131072 | tf_op jit(solution)/shard_map/all_to_all | solution.py:110
  48.5 16.0 %all-to-all-start = ((bf16[128,2,128]{2,1,0:T(2,128)(2,1)}), bf16[128,2,128]{2,1,0:T(2,128)(2,1)S(1)}, u32[]{:S(2)}, u32[]{:S(2)}) async-start(bf16[128,2,128]{2,1,0:T(2,128)(2,1)} %bitcast.18), calls=%async_computation | async-start | bytes 131072 | tf_op jit(solution)/shard_map/all_to_all | solution.py:111
  64.5 16.0 %all-to-all-start.2 = ((bf16[128,2,128]{2,1,0:T(2,128)(2,1)}), bf16[128,2,128]{2,1,0:T(2,128)(2,1)S(1)}, u32[]{:S(2)}, u32[]{:S(2)}) async-start(bf16[128,2,128]{2,1,0:T(2,128)(2,1)} %bitcast.43), calls=%async_computation.2 | async-start | bytes 131072 | tf_op jit(solution)/shard_map/all_to_all | solution.py:109
  84.2 16.0 %all-to-all-start.6 = ((bf16[2,128,128]{2,0,1:T(2,128)(2,1)}), bf16[2,128,128]{2,0,1:T(2,128)(2,1)S(1)}, u32[]{:S(2)}, u32[]{:S(2)}) async-start(bf16[2,128,128]{2,0,1:T(2,128)(2,1)} %copy.86), calls=%async_computation.6 | async-start | bytes 131072 | tf_op jit(solution)/shard_map/all_to_all | solution.py:125
  100.2 211.8 %all-to-all-start.5 = ((bf16[2,128,128]{2,0,1:T(2,128)(2,1)}), bf16[2,128,128]{2,0,1:T(2,128)(2,1)S(1)}, u32[]{:S(2)}, u32[]{:S(2)}) async-start(bf16[2,128,128]{2,0,1:T(2,128)(2,1)} %copy.79), calls=%async_computation.5 | async-start | bytes 131072 | tf_op jit(solution)/shard_map/all_to_all | solution.py:124
  106.1 204.3 %reduce-scatter.4.cloned.1.call-start = ((), (), s32[]{:S(2)}) async-start(), calls=%async_computation.8 | async-start | bytes 5242880
  312.0 17.7 %all-to-all-start.3 = ((bf16[2,128,128]{2,0,1:T(2,128)(2,1)}), bf16[2,128,128]{2,0,1:T(2,128)(2,1)S(1)}, u32[]{:S(2)}, u32[]{:S(2)}) async-start(bf16[2,128,128]{2,0,1:T(2,128)(2,1)} %copy.76), calls=%async_computation.3 | async-start | bytes 131072 | tf_op jit(solution)/shard_map/all_to_all | solution.py:123
Sparse Core Ops, SparseCore 0:
  114.7 167.5 reduce-scatter.3
where the time goes:
time: 338 us; the launch traced here: 337 us
  blocking collectives  195 us (58%)
  starting transfers between devices  51 us (15%)
  waiting for transfers between devices  47.7 us (14%)
  local copies, waits for them, and re-layouts  21.3 us (6%)
  between operations  14.2 us (4%)
  other arithmetic  4.09 us (1%)
  matrix products  3.94 us (1%)
    psum x1, blocking collectives, per_device(): skip_grad = lax.psum(placed, ('dp', 'context')) * scale  195 us
    unnamed x9, local copies, waits for them, and re-layouts  17.5 us
    all_to_all x1, starting transfers between devices, per_device(): lax.all_to_all(gate_in.T, 'context', split_axis=0, concat_axis=1, tiled=T...  13.8 us
    all_to_all x1, waiting for transfers between devices, per_device(): lax.all_to_all(grad_out_cols, 'context', split_axis=1, concat_axis=0, til...  9.03 us
    all_to_all x1, waiting for transfers between devices, per_device(): lax.all_to_all(value_rows.T, 'context', split_axis=0, concat_axis=1, tile...  8.14 us
    all_to_all x1, waiting for transfers between devices, per_device(): lax.all_to_all(gate_in.T, 'context', split_axis=0, concat_axis=1, tiled=T...  8.11 us
    all_to_all x1, waiting for transfers between devices, per_device(): lax.all_to_all(grad_in_cols, 'context', split_axis=1, concat_axis=0, tile...  7.85 us
    all_to_all x1, starting transfers between devices, per_device(): lax.all_to_all(grad_in_cols, 'context', split_axis=1, concat_axis=0, tile...  7.72 us
  transfers between devices with their start and end apart: 8, of which 6 were waited for; matrix products, arithmetic and copies ran while one was open for 7% of the time, Pallas kernels for 0%

commit v1 on v0

v1 whole, which is shorter than its diff:
```python
import functools
import math

import jax
import jax.numpy as jnp
import numpy as np
from jax import lax
from jax.experimental import pallas as pl
from jax.experimental.pallas import tpu as pltpu
from jax.sharding import PartitionSpec as P

MESH = pl.DeviceIdType.MESH
F32 = jnp.float32
BF16 = jnp.bfloat16


def group_sizes(context):
    near = 1
    while 2 * near * near * 2 <= context:
        near *= 2
    return context // near, near


def dft_tables(pieces, block_len, rows, scale):
    outer = 2 * pieces
    total = outer * block_len

    def angle(first, second, modulus):
        return (first[:, None] * second[None, :] % modulus) * (2.0 * math.pi / modulus)

    across = np.arange(pieces)
    outer_index = np.arange(outer)
    inner_index = np.arange(block_len)
    first = angle(outer_index, across, outer)
    entry = np.concatenate([np.cos(first), -np.sin(first)], 0)
    twist = angle(outer_index, inner_index, total)
    twist_cos, twist_sin = np.cos(twist), np.sin(twist)
    inner = angle(inner_index, inner_index, block_len)
    cosine, sine = np.cos(inner), np.sin(inner)
    forward_inner = np.block([[cosine, -sine], [sine, cosine]])
    inverse_inner = np.block([[cosine, sine], [-sine, cosine]])
    last = angle(across, outer_index, outer)
    leave = np.concatenate([np.cos(last), -np.sin(last)], 1) * scale

    def low(table):
        return jnp.asarray(table.astype(np.float32), dtype=BF16)

    return (
        low(entry[:, rows]),
        low(entry),
        jnp.asarray(twist_cos.astype(np.float32)),
        jnp.asarray(twist_sin.astype(np.float32)),
        low(forward_inner),
        low(inverse_inner),
        low(leave[rows]),
        low(leave),
    )


def dot(a, b):
    return jnp.dot(a, b, preferred_element_type=F32)


def flip(x):
    n = x.shape[1]
    eye = (
        lax.broadcasted_iota(jnp.int32, (n, n), 0) == lax.broadcasted_iota(jnp.int32, (n, n), 1)
    ).astype(BF16)
    return lax.dot_general(
        eye, x, (((1,), (1,)), ((), ())), preferred_element_type=F32
    ).astype(BF16)


def regroup(x, outer, inner):
    n = outer * inner
    row = lax.broadcasted_iota(jnp.int32, (n, n), 0)
    col = lax.broadcasted_iota(jnp.int32, (n, n), 1)
    place = (col == (row % outer) * inner + row // outer).astype(BF16)
    return dot(place, x).astype(BF16)


def mixer_kernel(
    sizes,
    ig_hbm, va_hbm, og_hbm, go_hbm, taps_hbm, entry_hbm, entry_nat_hbm, cos_hbm, sin_hbm,
    fwd_hbm, inv_hbm, leave_hbm, leave_nat_hbm,
    conv_ref, back_ref, filter_ref, skip_ref,
    ig, va, og, go, taps, entry, entry_nat, cos, sin, fwd, inv, leave, leave_nat,
    send1, recv1, send2, recv2, send3, recv3, send4, recv4,
    fsend, frecv, sdp, sdp_recv, s3, s3_recv, s4, s4_recv, kern,
    load_sem, send_sem, recv_sem,
):
    n_dp, far, near, chans, block = sizes
    ctx = far * near
    outer = 2 * ctx
    d = lax.axis_index("dp")
    c = lax.axis_index("context")
    g = c // near
    h = c % near

    pairs = (
        (ig_hbm, ig), (va_hbm, va), (og_hbm, og), (go_hbm, go), (taps_hbm, taps),
        (entry_nat_hbm, entry_nat), (cos_hbm, cos), (sin_hbm, sin), (fwd_hbm, fwd),
        (entry_hbm, entry), (inv_hbm, inv), (leave_hbm, leave), (leave_nat_hbm, leave_nat),
    )
    loads = [pltpu.make_async_copy(src, dst, load_sem.at[i]) for i, (src, dst) in enumerate(pairs)]
    for load in loads:
        load.start()

    def far_peer(i):
        t = (g + i) % far
        return t, (d, t * near + h)

    def near_peer(i):
        t = (h + i) % near
        return t, (d, g * near + t)

    def dp_peer(i):
        t = (d + i) % n_dp
        return t, (t, c)

    barrier = pltpu.get_barrier_semaphore()

    def greet(peer):
        def step(i, carry):
            pl.semaphore_signal(barrier, inc=1, device_id=peer(i)[1], device_id_type=MESH)
            return carry

        return step

    lax.fori_loop(1, far, greet(far_peer), 0)
    lax.fori_loop(1, near, greet(near_peer), 0)
    lax.fori_loop(1, n_dp, greet(dp_peer), 0)

    def send_all(peer, count, src, dst, own, sem):
        def step(i, carry):
            t, target = peer(i)
            pltpu.make_async_remote_copy(
                src_ref=src(t),
                dst_ref=dst.at[own],
                send_sem=send_sem.at[sem],
                recv_sem=recv_sem.at[sem],
                device_id=target,
                device_id_type=MESH,
            ).start()
            return carry

        lax.fori_loop(1, count, step, 0)

    def wait_blocks(dst, count, sem):
        part = dst.at[pl.ds(0, count - 1)]
        pltpu.make_async_copy(part, part, sem).wait()

    for i in range(4):
        loads[i].wait()
    mixed = (ig[...].astype(F32) * va[...].astype(F32)).astype(BF16)
    gmix = (go[...].astype(F32) * og[...].astype(F32)).astype(BF16)
    cols = flip(jnp.concatenate([mixed, gmix], 0))
    send1[:, 0] = cols[:, :block].reshape(far, 2 * near, block)
    send1[:, 1] = cols[:, block:].reshape(far, 2 * near, block)
    recv1[g] = send1[g]

    pl.semaphore_wait(barrier, far + near + n_dp - 3)
    send_all(far_peer, far, lambda t: send1.at[t], recv1, g, 0)

    def forward(table, x):
        section = dot(table, x)
        out = []
        for i in range(x.shape[1] // block):
            re = section[:outer, i * block : (i + 1) * block]
            im = section[outer:, i * block : (i + 1) * block]
            turned = jnp.concatenate(
                [
                    (re * cos[...] + im * sin[...]).astype(BF16),
                    (im * cos[...] - re * sin[...]).astype(BF16),
                ],
                1,
            )
            out.append(dot(turned, fwd[...]))
        return out

    def inverse(table, spectra):
        real, imag = [], []
        for spectrum in spectra:
            back = dot(spectrum, inv[...])
            re, im = back[:, :block], back[:, block:]
            real.append((re * cos[...] - im * sin[...]).astype(BF16))
            imag.append((im * cos[...] + re * sin[...]).astype(BF16))
        turned = jnp.concatenate([jnp.concatenate(real, 1), jnp.concatenate(imag, 1)], 0)
        return dot(table, turned)

    for i in range(4, 9):
        loads[i].wait()
    for j, spectrum in enumerate(
        forward(entry_nat[...], jnp.concatenate([taps[0], taps[1]], 1))
    ):
        kern[j] = spectrum

    wait_blocks(recv1, far, recv_sem.at[0])
    rows = jnp.concatenate(
        [recv1[:, 0].reshape(chans, block), recv1[:, 1].reshape(chans, block)], 1
    )
    rows = regroup(rows, far, 2 * near)
    send2[:, 0] = rows[:, :block].reshape(near, 2, far, block)
    send2[:, 1] = rows[:, block:].reshape(near, 2, far, block)
    recv2[h] = send2[h]
    send_all(near_peer, near, lambda t: send2.at[t], recv2, h, 1)

    for i in range(9, 13):
        loads[i].wait()
    wait_blocks(recv2, near, recv_sem.at[1])

    halves = []
    for j in range(2):
        a = recv2[:, 0, j].reshape(ctx, block)
        b = recv2[:, 1, j].reshape(ctx, block)
        halves.append((a, b))
        sdp[pl.ds(j, 1)] = jnp.sum(a.astype(F32) * b.astype(F32), axis=0, keepdims=True)
    sdp_recv[d] = sdp[...]
    send_all(dp_peer, n_dp, lambda t: sdp, sdp_recv, d, 2)

    filter_specs = []
    for j in range(2):
        u, v = forward(entry[...], jnp.concatenate(halves[j], 1))
        k = kern[j]
        ur, ui = u[:, :block], u[:, block:]
        vr, vi = v[:, :block], v[:, block:]
        kr, ki = k[:, :block], k[:, block:]
        conv = jnp.concatenate([ur * kr - ui * ki, ur * ki + ui * kr], 1).astype(BF16)
        back = jnp.concatenate([kr * vr + ki * vi, kr * vi - ki * vr], 1).astype(BF16)
        filter_specs.append(
            jnp.concatenate([ur * vr + ui * vi, ur * vi - ui * vr], 1).astype(BF16)
        )
        both = inverse(leave[...], [conv, back]).astype(BF16)
        send3[:, 0, j] = both[:, :block].reshape(near, far, block)
        send3[:, 1, j] = both[:, block:].reshape(near, far, block)
    recv3[h] = send3[h]
    send_all(near_peer, near, lambda t: send3.at[t], recv3, h, 3)

    wait_blocks(sdp_recv, n_dp, recv_sem.at[2])
    total = sdp_recv[0]
    for i in range(1, n_dp):
        total = total + sdp_recv[i]
    total = jnp.sum(total, axis=1, keepdims=True) * (1.0 / math.sqrt(n_dp * ctx * block))
    channel = lax.broadcasted_iota(jnp.int32, (2, 128), 0) * 128 + lax.broadcasted_iota(
        jnp.int32, (2, 128), 1
    )
    zero = jnp.zeros((2, 128), F32)
    s3[...] = jnp.where(channel == 2 * c, total[0:1], zero) + jnp.where(
        channel == 2 * c + 1, total[1:2], zero
    )
    s3_recv[h] = s3[...]
    send_all(near_peer, near, lambda t: s3, s3_recv, h, 4)

    term = inverse(leave_nat[...], filter_specs).astype(BF16)
    fsend[:, 0] = term[:, :block].reshape(n_dp, ctx // n_dp, block)
    fsend[:, 1] = term[:, block:].reshape(n_dp, ctx // n_dp, block)
    frecv[d] = fsend[d]
    send_all(dp_peer, n_dp, lambda t: fsend.at[t], frecv, d, 5)

    wait_blocks(recv3, near, recv_sem.at[3])
    rows = jnp.concatenate(
        [recv3[:, 0].reshape(chans, block), recv3[:, 1].reshape(chans, block)], 1
    )
    rows = regroup(rows, 2 * near, far)
    send4[:, 0] = rows[:, :block].reshape(far, 2 * near, block)
    send4[:, 1] = rows[:, block:].reshape(far, 2 * near, block)
    recv4[g] = send4[g]
    send_all(far_peer, far, lambda t: send4.at[t], recv4, g, 6)

    wait_blocks(s3_recv, near, recv_sem.at[4])
    total = s3_recv[0]
    for i in range(1, near):
        total = total + s3_recv[i]
    s4[...] = total
    s4_recv[g] = total
    send_all(far_peer, far, lambda t: s4, s4_recv, g, 7)

    wait_blocks(frecv, n_dp, recv_sem.at[5])
    grad = frecv[0].astype(F32)
    for i in range(1, n_dp):
        grad = grad + frecv[i].astype(F32)
    filter_ref[...] = grad * (1.0 / math.sqrt(n_dp * ctx * block))

    wait_blocks(recv4, far, recv_sem.at[6])
    tokens = flip(
        jnp.concatenate(
            [recv4[:, 0].reshape(chans, block), recv4[:, 1].reshape(chans, block)], 1
        )
    )
    conv_ref[...] = tokens[:block]
    back_ref[...] = tokens[block:]

    wait_blocks(s4_recv, far, recv_sem.at[7])
    total = s4_recv[0]
    for i in range(1, far):
        total = total + s4_recv[i]
    skip_ref[...] = total

    wait_blocks(recv1, far, send_sem.at[0])
    wait_blocks(recv2, near, send_sem.at[1])
    wait_blocks(sdp_recv, n_dp, send_sem.at[2])
    wait_blocks(recv3, near, send_sem.at[3])
    wait_blocks(s3_recv, near, send_sem.at[4])
    wait_blocks(frecv, n_dp, send_sem.at[5])
    wait_blocks(recv4, far, send_sem.at[6])
    wait_blocks(s4_recv, far, send_sem.at[7])


def per_device(input_gate, values, output_gate, grad_out, filter_taps, skip_gain):
    n_dp = lax.axis_size("dp")
    ctx = lax.axis_size("context")
    far, near = group_sizes(ctx)
    block, chans = input_gate.shape[1:]
    rows = np.arange(ctx).reshape(far, near).T.reshape(-1)
    tables = dft_tables(ctx, block, rows, 1.0 / (2 * ctx * block))
    gates = (input_gate[0], values[0], output_gate[0], grad_out[0])
    operands = gates + (filter_taps.reshape(-1, ctx, block),) + tables
    share = ctx // n_dp
    outs = (
        jax.ShapeDtypeStruct((block, chans), BF16),
        jax.ShapeDtypeStruct((block, chans), BF16),
        jax.ShapeDtypeStruct((2, share, block), F32),
        jax.ShapeDtypeStruct((2, 128), F32),
    )
    vmem = pltpu.VMEM
    conv_out, conv_back, filter_grad, skip_grad = pl.pallas_call(
        functools.partial(mixer_kernel, (n_dp, far, near, chans, block)),
        out_shape=outs,
        in_specs=[pl.BlockSpec(memory_space=pl.ANY)] * len(operands),
        out_specs=tuple(pl.BlockSpec(memory_space=pltpu.VMEM) for _ in outs),
        scratch_shapes=[vmem(x.shape, x.dtype) for x in operands]
        + [vmem((far, 2, 2 * near, block), BF16)] * 2
        + [vmem((near, 2, 2, far, block), BF16)] * 4
        + [vmem((far, 2, 2 * near, block), BF16)] * 2
        + [vmem((n_dp, 2, share, block), BF16)] * 2
        + [vmem((2, block), F32), vmem((n_dp, 2, block), F32)]
        + [vmem((2, 128), F32), vmem((near, 2, 128), F32)]
        + [vmem((2, 128), F32), vmem((far, 2, 128), F32)]
        + [vmem((2, 2 * ctx, 2 * block), F32)]
        + [
            pltpu.SemaphoreType.DMA((len(operands),)),
            pltpu.SemaphoreType.DMA((8,)),
            pltpu.SemaphoreType.DMA((8,)),
        ],
        compiler_params=pltpu.CompilerParams(
            collective_id=0, has_side_effects=True, vmem_limit_bytes=48 * 1024 * 1024
        ),
        name="mixer",
    )(*operands)

    gate_in, value, gate_out, cotangent = (x.astype(F32) for x in gates)
    mixed = (gate_in * value).astype(BF16).astype(F32)
    grad_mix = (cotangent * gate_out).astype(BF16).astype(F32)
    grad_output = (cotangent * (conv_out.astype(F32) + skip_gain * mixed)).astype(BF16)
    grad_mixed = conv_back.astype(F32) + skip_gain * grad_mix
    grad_input = (grad_mixed * value).astype(BF16)
    grad_value = (grad_mixed * gate_in).astype(BF16)
    return (
        grad_input[None],
        grad_value[None],
        grad_output[None],
        filter_grad.reshape(2, share * block),
        skip_grad.reshape(-1)[:chans],
    )


def solution(mesh):
    return jax.shard_map(
        per_device,
        mesh=mesh,
        in_specs=(
            P("dp", "context", None),
            P("dp", "context", None),
            P("dp", "context", None),
            P("dp", "context", None),
            P("context", None),
            P(),
        ),
        out_specs=(
            P("dp", "context", None),
            P("dp", "context", None),
            P("dp", "context", None),
            P("context", "dp"),
            P(),
        ),
        check_vma=False,
    )
```

time: 338 us -> 57.5 us (0.17)
  blocking collectives: 195 us -> 0 us
  starting transfers between devices: 51 us -> 0 us
  waiting for transfers between devices: 47.7 us -> 0 us
  Pallas kernels: 0 us -> 43.3 us
  between operations: 14.2 us -> 0.69 us
  local copies, waits for them, and re-layouts: 21.3 us -> 11.7 us
  matrix products: 3.94 us -> 0 us
    psum x1 -> x0, blocking collectives: 195 us -> none  [per_device(): skip_grad = lax.psum(placed, ('dp', 'context')) * scale]
    all_to_all x7 -> x0, starting transfers between devices: 51 us -> none  [the longest x1 13.8 us: per_device(): lax.all_to_all(gate_in.T, 'context', split_axis=0, concat_axis=1, tiled=T...]
    all_to_all x7 -> x0, waiting for transfers between devices: 47.7 us -> none  [the longest x1 9.03 us: per_device(): lax.all_to_all(grad_out_cols, 'context', split_axis=1, concat_axis=0, til...]
    pallas_call x0 -> x1, Pallas kernels: none -> 43.3 us  [per_device(): pl.pallas_call(functools.partial(mixer_kernel, (n_dp, far, near, chans, b...]
    unnamed x9 -> x29, local copies, waits for them, and re-layouts: 17.5 us -> 11.7 us
    dot_general x12 -> x0, matrix products: 3.94 us -> none  [the longest x3 1.51 us: transform(): jnp.einsum('pka,rab->prkb', entry, shaped, preferred_element_type=jnp.flo...]
  transfers between devices with their start and end apart: 8 -> 0, of which waited for: 6 -> 0; matrix products, arithmetic and copies ran while one was open for 7% -> 0% of each run, Pallas kernels for 0% -> 0%
where the time goes in v1:
time: 57.5 us; the launch traced here: 56.4 us
  Pallas kernels  43.3 us (75%)
  local copies, waits for them, and re-layouts  11.7 us (20%)
  other arithmetic  0.74 us (1%)
  between operations  0.69 us (1%)
    pallas_call x1, Pallas kernels, per_device(): pl.pallas_call(functools.partial(mixer_kernel, (n_dp, far, near, chans, b...  43.3 us
    unnamed x29, local copies, waits for them, and re-layouts  11.7 us

profile of v1, /device:TPU:1, one launch (start us, length us, event | category | flops | bytes accessed | tf_op | source)
XLA Modules:
  0.0 56.4 jit_solution(9527456718223634066)
XLA Ops:
  0.6 0.0 copy-start
  0.6 0.0 copy-start.1
  0.7 0.9 %copy.23 = bf16[1,2,128,128]{3,2,1,0:T(8,128)(2,1)S(1)} copy(bf16[1,2,128,128]{3,1,2,0:T(2,128)(2,1)} %bitcast.35) | data formatting | bytes 131072
  1.5 0.0 copy-done
  1.5 0.0 copy-done.1
  1.6 0.0 copy-start.2
  1.6 0.8 %copy-done.2 = bf16[1,128,256]{2,1,0:T(8,128)(2,1)S(1)} copy-done((bf16[1,128,256]{2,1,0:T(8,128)(2,1)S(1)}, bf16[1,128,256]{2,1,0:T(8,128)(2,1)}, u32[]{:S(2)}) %copy-start.2) | copy-done | bytes 65560
  2.4 0.0 copy-start.3
  2.4 0.8 %copy-done.3 = bf16[1,128,256]{2,1,0:T(8,128)(2,1)S(1)} copy-done((bf16[1,128,256]{2,1,0:T(8,128)(2,1)S(1)}, bf16[1,128,256]{2,1,0:T(8,128)(2,1)}, u32[]{:S(2)}) %copy-start.3) | copy-done | bytes 65560
  3.2 0.0 copy-start.4
  3.2 0.9 %copy-done.4 = bf16[128,512]{1,0:T(8,128)(2,1)S(1)} copy-done((bf16[128,512]{1,0:T(8,128)(2,1)S(1)}, bf16[128,512]{1,0:T(8,128)(2,1)}, u32[]{:S(2)}) %copy-start.4) | copy-done | bytes 131096
  4.1 0.0 copy-start.5
  4.1 0.9 %copy-done.5 = bf16[128,512]{1,0:T(8,128)(2,1)S(1)} copy-done((bf16[128,512]{1,0:T(8,128)(2,1)S(1)}, bf16[128,512]{1,0:T(8,128)(2,1)}, u32[]{:S(2)}) %copy-start.5) | copy-done | bytes 131096
  5.1 0.9 %copy-done.6 = bf16[256,256]{1,0:T(8,128)(2,1)S(1)} copy-done((bf16[256,256]{1,0:T(8,128)(2,1)S(1)}, bf16[256,256]{1,0:T(8,128)(2,1)}, u32[]{:S(2)}) %copy-start.6) | copy-done | bytes 131096
  6.0 0.9 %copy-done.7 = bf16[256,256]{1,0:T(8,128)(2,1)S(1)} copy-done((bf16[256,256]{1,0:T(8,128)(2,1)S(1)}, bf16[256,256]{1,0:T(8,128)(2,1)}, u32[]{:S(2)}) %copy-start.7) | copy-done | bytes 131096
  6.9 0.9 %copy-done.8 = f32[256,128]{1,0:T(8,128)S(1)} copy-done((f32[256,128]{1,0:T(8,128)S(1)}, f32[256,128]{1,0:T(8,128)}, u32[]{:S(2)}) %copy-start.8) | copy-done | bytes 131096
  7.8 0.9 %copy-done.9 = f32[256,128]{1,0:T(8,128)S(1)} copy-done((f32[256,128]{1,0:T(8,128)S(1)}, f32[256,128]{1,0:T(8,128)}, u32[]{:S(2)}) %copy-start.9) | copy-done | bytes 131096
  8.7 0.9 %copy-done.10 = bf16[512,128]{1,0:T(8,128)(2,1)S(1)} copy-done((bf16[512,128]{1,0:T(8,128)(2,1)S(1)}, bf16[512,128]{1,0:T(8,128)(2,1)}, u32[]{:S(2)}) %copy-start.10) | copy-done | bytes 131096
  9.6 0.9 %copy-done.11 = bf16[512,128]{1,0:T(8,128)(2,1)S(1)} copy-done((bf16[512,128]{1,0:T(8,128)(2,1)S(1)}, bf16[512,128]{1,0:T(8,128)(2,1)}, u32[]{:S(2)}) %copy-start.11) | copy-done | bytes 131096
  10.5 43.3 %mixer.1 = (bf16[128,256]{1,0:T(8,128)(2,1)S(1)}, bf16[128,256]{1,0:T(8,128)(2,1)S(1)}, f32[2,32,128]{2,1,0:T(8,128)S(1)}, f32[2,128]{1,0:T(2,128)S(1)}) custom-call(bf16[128,256]{1,0:T(8,128)(2,1)S(1)} %bitcast.28, bf16[128,256]{1,0:T(8,128)(2,1)S(1)} %bitcast.29, bf16[128,256]{1,0:T(8,128)(2,1)S(1)} %bitcast.30, bf16[128,256]{1,0:T(8,128)(2,1)S(1)} %bitcast.31, ...), custom_call_target="tpu_custom_call" | custom-call | tf_op jit(solution)/shard_map/mixer/pallas_call | solution.py:326
  53.8 0.6 %copy.24 = f32[1,2,32,128]{3,1,2,0:T(2,128)} copy(f32[1,2,32,128]{3,2,1,0:T(8,128)S(1)} %bitcast.33) | data formatting | bytes 65536
  54.4 0.7 %copy-done.12 = f32[256]{0:T(256)S(1)} copy-done((f32[256]{0:T(256)S(1)}, f32[256]{0:T(256)}, u32[]{:S(2)}) %copy-start.12) | copy-done | bytes 1048
  55.1 0.7 %fusion.5 = (bf16[1,128,256]{2,1,0:T(8,128)(2,1)}, bf16[1,128,256]{2,1,0:T(8,128)(2,1)}, bf16[1,128,256]{2,1,0:T(8,128)(2,1)}) fusion(bf16[128,256]{1,0:T(8,128)(2,1)S(1)} %get-tuple-element.9, f32[256]{0:T(256)S(1)} %copy-done.12, bf16[1,128,256]{2,1,0:T(8,128)(2,1)S(1)} %copy-done.3, bf16[1,128,256]{2,1,0:T(8,128)(2,1)S(1)} %copy-done.2, ...), kind=kLoop, calls=%fused_computation.11 | loop fusion | flops 720896 | bytes 590848 | tf_op jit(solution)/shard_map/broadcast_in_dim | solution.py:360
  55.9 0.6 copy.26
  (7 shorter events, 0.0 us)
Async XLA Ops:
  0.6 0.9 %copy-start = (bf16[1,128,256]{2,1,0:T(8,128)(2,1)S(1)}, bf16[1,128,256]{2,1,0:T(8,128)(2,1)}, u32[]{:S(2)}) copy-start(bf16[1,128,256]{2,1,0:T(8,128)(2,1)} %param.14) | copy-start | bytes 196612
  0.6 0.9 %copy-start.1 = (bf16[1,128,256]{2,1,0:T(8,128)(2,1)S(1)}, bf16[1,128,256]{2,1,0:T(8,128)(2,1)}, u32[]{:S(2)}) copy-start(bf16[1,128,256]{2,1,0:T(8,128)(2,1)} %param.15) | copy-start | bytes 196612
  1.6 0.8 %copy-start.2 = (bf16[1,128,256]{2,1,0:T(8,128)(2,1)S(1)}, bf16[1,128,256]{2,1,0:T(8,128)(2,1)}, u32[]{:S(2)}) copy-start(bf16[1,128,256]{2,1,0:T(8,128)(2,1)} %param.16) | copy-start | bytes 196612
  2.4 0.8 %copy-start.3 = (bf16[1,128,256]{2,1,0:T(8,128)(2,1)S(1)}, bf16[1,128,256]{2,1,0:T(8,128)(2,1)}, u32[]{:S(2)}) copy-start(bf16[1,128,256]{2,1,0:T(8,128)(2,1)} %param.17) | copy-start | bytes 196612
  3.2 0.9 %copy-start.4 = (bf16[128,512]{1,0:T(8,128)(2,1)S(1)}, bf16[128,512]{1,0:T(8,128)(2,1)}, u32[]{:S(2)}) copy-start(bf16[128,512]{1,0:T(8,128)(2,1)} %constant.23.clone.leave_nat_hbm) | copy-start | bytes 393220
  4.1 0.9 %copy-start.5 = (bf16[128,512]{1,0:T(8,128)(2,1)S(1)}, bf16[128,512]{1,0:T(8,128)(2,1)}, u32[]{:S(2)}) copy-start(bf16[128,512]{1,0:T(8,128)(2,1)} %constant.22.clone.leave_hbm) | copy-start | bytes 393220
  5.1 0.9 %copy-start.6 = (bf16[256,256]{1,0:T(8,128)(2,1)S(1)}, bf16[256,256]{1,0:T(8,128)(2,1)}, u32[]{:S(2)}) copy-start(bf16[256,256]{1,0:T(8,128)(2,1)} %constant.21.clone.inv_hbm) | copy-start | bytes 393220
  6.0 0.9 %copy-start.7 = (bf16[256,256]{1,0:T(8,128)(2,1)S(1)}, bf16[256,256]{1,0:T(8,128)(2,1)}, u32[]{:S(2)}) copy-start(bf16[256,256]{1,0:T(8,128)(2,1)} %constant.20.clone.fwd_hbm) | copy-start | bytes 393220
  6.9 0.9 %copy-start.8 = (f32[256,128]{1,0:T(8,128)S(1)}, f32[256,128]{1,0:T(8,128)}, u32[]{:S(2)}) copy-start(f32[256,128]{1,0:T(8,128)} %constant.19.clone.sin_hbm) | copy-start | bytes 393220
  7.8 0.9 %copy-start.9 = (f32[256,128]{1,0:T(8,128)S(1)}, f32[256,128]{1,0:T(8,128)}, u32[]{:S(2)}) copy-start(f32[256,128]{1,0:T(8,128)} %constant.18.clone.cos_hbm) | copy-start | bytes 393220
  8.7 0.9 %copy-start.10 = (bf16[512,128]{1,0:T(8,128)(2,1)S(1)}, bf16[512,128]{1,0:T(8,128)(2,1)}, u32[]{:S(2)}) copy-start(bf16[512,128]{1,0:T(8,128)(2,1)} %constant.17.clone.entry_nat_hbm) | copy-start | bytes 393220
  9.6 0.9 %copy-start.11 = (bf16[512,128]{1,0:T(8,128)(2,1)S(1)}, bf16[512,128]{1,0:T(8,128)(2,1)}, u32[]{:S(2)}) copy-start(bf16[512,128]{1,0:T(8,128)(2,1)} %constant.16.clone.entry_hbm) | copy-start | bytes 393220
  54.4 0.7 %copy-start.12 = (f32[256]{0:T(256)S(1)}, f32[256]{0:T(256)}, u32[]{:S(2)}) copy-start(f32[256]{0:T(256)} %param.19) | copy-start | bytes 3076

commit v2 on v1

--- a/solution.py
+++ b/solution.py
@@ -12,6 +12,7 @@
 MESH = pl.DeviceIdType.MESH
 F32 = jnp.float32
 BF16 = jnp.bfloat16
+UNROLL = False
 
 
 def group_sizes(context):
@@ -43,14 +44,14 @@
     leave = np.concatenate([np.cos(last), -np.sin(last)], 1) * scale
 
     def low(table):
-        return jnp.asarray(table.astype(np.float32), dtype=BF16)
+        return table.astype(BF16).astype(np.float32)
 
     return (
+        low(entry),
+        twist_cos.astype(np.float32),
+        twist_sin.astype(np.float32),
+        low(forward_inner),
         low(entry[:, rows]),
-        low(entry),
-        jnp.asarray(twist_cos.astype(np.float32)),
-        jnp.asarray(twist_sin.astype(np.float32)),
-        low(forward_inner),
         low(inverse_inner),
         low(leave[rows]),
         low(leave),
@@ -81,12 +82,13 @@
 
 def mixer_kernel(
     sizes,
-    ig_hbm, va_hbm, og_hbm, go_hbm, taps_hbm, entry_hbm, entry_nat_hbm, cos_hbm, sin_hbm,
-    fwd_hbm, inv_hbm, leave_hbm, leave_nat_hbm,
+    ig_hbm, va_hbm, og_hbm, go_hbm, taps_hbm, entry_nat_hbm, cos_hbm, sin_hbm, fwd_hbm,
+    entry_hbm, inv_hbm, leave_hbm, leave_nat_hbm,
     conv_ref, back_ref, filter_ref, skip_ref,
-    ig, va, og, go, taps, entry, entry_nat, cos, sin, fwd, inv, leave, leave_nat,
+    ig, va, og, go, taps, entry_nat_in, cos, sin, fwd_in, entry_in, inv_in, leave_in,
+    leave_nat_in, taps_rows, entry_nat, fwd, entry, inv, leave, leave_nat,
     send1, recv1, send2, recv2, send3, recv3, send4, recv4,
-    fsend, frecv, sdp, sdp_recv, s3, s3_recv, s4, s4_recv, kern,
+    fsend, frecv, near_sum, near_recv, far_sum, far_recv, dp_sum, dp_recv, kern,
     load_sem, send_sem, recv_sem,
 ):
     n_dp, far, near, chans, block = sizes
@@ -99,23 +101,24 @@
 
     pairs = (
         (ig_hbm, ig), (va_hbm, va), (og_hbm, og), (go_hbm, go), (taps_hbm, taps),
-        (entry_nat_hbm, entry_nat), (cos_hbm, cos), (sin_hbm, sin), (fwd_hbm, fwd),
-        (entry_hbm, entry), (inv_hbm, inv), (leave_hbm, leave), (leave_nat_hbm, leave_nat),
+        (entry_nat_hbm, entry_nat_in), (cos_hbm, cos), (sin_hbm, sin), (fwd_hbm, fwd_in),
+        (entry_hbm, entry_in), (inv_hbm, inv_in), (leave_hbm, leave_in),
+        (leave_nat_hbm, leave_nat_in),
     )
     loads = [pltpu.make_async_copy(src, dst, load_sem.at[i]) for i, (src, dst) in enumerate(pairs)]
     for load in loads:
         load.start()
 
     def far_peer(i):
-        t = (g + i) % far
+        t = lax.rem(g + i, far)
         return t, (d, t * near + h)
 
     def near_peer(i):
-        t = (h + i) % near
+        t = lax.rem(h + i, near)
         return t, (d, g * near + t)
 
     def dp_peer(i):
-        t = (d + i) % n_dp
+        t = lax.rem(d + i, n_dp)
         return t, (t, c)
 
     barrier = pltpu.get_barrier_semaphore()
@@ -129,7 +132,8 @@
 
     lax.fori_loop(1, far, greet(far_peer), 0)
     lax.fori_loop(1, near, greet(near_peer), 0)
-    lax.fori_loop(1, n_dp, greet(dp_peer), 0)
+    half = n_dp // 2
+    ahead = d + (d // half) * (half - 1 - 2 * lax.rem(d, half))
 
     def send_all(peer, count, src, dst, own, sem):
         def step(i, carry):
@@ -144,11 +148,11 @@
             ).start()
             return carry
 
-        lax.fori_loop(1, count, step, 0)
-
-    def wait_blocks(dst, count, sem):
+        lax.fori_loop(1, count, step, 0, unroll=UNROLL)
+
+    def wait_blocks(dst, count, sems, i):
         part = dst.at[pl.ds(0, count - 1)]
-        pltpu.make_async_copy(part, part, sem).wait()
+        pltpu.make_async_copy(part, part, sems.at[i]).wait()
 
     for i in range(4):
         loads[i].wait()
@@ -158,9 +162,13 @@
     send1[:, 0] = cols[:, :block].reshape(far, 2 * near, block)
     send1[:, 1] = cols[:, block:].reshape(far, 2 * near, block)
     recv1[g] = send1[g]
-
-    pl.semaphore_wait(barrier, far + near + n_dp - 3)
+    near_sum[...] = jnp.sum(mixed.astype(F32) * gmix.astype(F32), axis=0, keepdims=True)
+    near_recv[h] = near_sum[...]
+
+    pl.semaphore_wait(barrier, far + near - 2 + ahead)
+    lax.fori_loop(1, n_dp, greet(dp_peer), 0)
     send_all(far_peer, far, lambda t: send1.at[t], recv1, g, 0)
+    send_all(near_peer, near, lambda t: near_sum, near_recv, h, 4)
 
     def forward(table, x):
         section = dot(table, x)
@@ -190,12 +198,16 @@
 
     for i in range(4, 9):
         loads[i].wait()
-    for j, spectrum in enumerate(
-        forward(entry_nat[...], jnp.concatenate([taps[0], taps[1]], 1))
-    ):
+    entry_nat[...] = entry_nat_in[...].astype(BF16)
+    fwd[...] = fwd_in[...].astype(BF16)
+    for j in range(2):
+        for a in range(ctx):
+            taps_rows[j, pl.ds(a, 1)] = taps[pl.ds(j, 1), pl.ds(a * block, block)].astype(F32)
+    both = jnp.concatenate([taps_rows[0], taps_rows[1]], 1).astype(BF16)
+    for j, spectrum in enumerate(forward(entry_nat[...], both)):
         kern[j] = spectrum
 
-    wait_blocks(recv1, far, recv_sem.at[0])
+    wait_blocks(recv1, far, recv_sem, 0)
     rows = jnp.concatenate(
         [recv1[:, 0].reshape(chans, block), recv1[:, 1].reshape(chans, block)], 1
     )
@@ -205,59 +217,64 @@
     recv2[h] = send2[h]
     send_all(near_peer, near, lambda t: send2.at[t], recv2, h, 1)
 
+    def total(blocks, count):
+        value = blocks[0]
+        for i in range(1, count):
+            value = value + blocks[i]
+        return value
+
+    wait_blocks(near_recv, near, recv_sem, 4)
+    far_sum[...] = total(near_recv, near)
+    far_recv[g] = far_sum[...]
+    send_all(far_peer, far, lambda t: far_sum, far_recv, g, 7)
+
     for i in range(9, 13):
         loads[i].wait()
-    wait_blocks(recv2, near, recv_sem.at[1])
-
-    halves = []
+    entry[...] = entry_in[...].astype(BF16)
+    inv[...] = inv_in[...].astype(BF16)
+    leave[...] = leave_in[...].astype(BF16)
+    leave_nat[...] = leave_nat_in[...].astype(BF16)
+    wait_blocks(recv2, near, recv_sem, 1)
+
+    sources, gradients = [], []
     for j in range(2):
-        a = recv2[:, 0, j].reshape(ctx, block)
-        b = recv2[:, 1, j].reshape(ctx, block)
-        halves.append((a, b))
-        sdp[pl.ds(j, 1)] = jnp.sum(a.astype(F32) * b.astype(F32), axis=0, keepdims=True)
-    sdp_recv[d] = sdp[...]
-    send_all(dp_peer, n_dp, lambda t: sdp, sdp_recv, d, 2)
-
-    filter_specs = []
+        halves = [recv2[:, i, j].reshape(ctx, block) for i in range(2)]
+        u, v = forward(entry[...], jnp.concatenate(halves, 1))
+        sources.append((u[:, :block], u[:, block:]))
+        gradients.append((v[:, :block], v[:, block:]))
+
+    specs = []
+    for (ur, ui), (vr, vi) in zip(sources, gradients):
+        specs.append(jnp.concatenate([ur * vr + ui * vi, ur * vi - ui * vr], 1).astype(BF16))
+    term = inverse(leave_nat[...], specs).astype(BF16)
+    fsend[:, 0] = term[:, :block].reshape(n_dp, ctx // n_dp, block)
+    fsend[:, 1] = term[:, block:].reshape(n_dp, ctx // n_dp, block)
+    frecv[d] = fsend[d]
+
+    @pl.when(ahead < n_dp - 1)
+    def _():
+        pl.semaphore_wait(barrier, n_dp - 1 - ahead)
+
+    send_all(dp_peer, n_dp, lambda t: fsend.at[t], frecv, d, 5)
+
     for j in range(2):
-        u, v = forward(entry[...], jnp.concatenate(halves[j], 1))
+        (ur, ui), (vr, vi) = sources[j], gradients[j]
         k = kern[j]
-        ur, ui = u[:, :block], u[:, block:]
-        vr, vi = v[:, :block], v[:, block:]
         kr, ki = k[:, :block], k[:, block:]
         conv = jnp.concatenate([ur * kr - ui * ki, ur * ki + ui * kr], 1).astype(BF16)
         back = jnp.concatenate([kr * vr + ki * vi, kr * vi - ki * vr], 1).astype(BF16)
-        filter_specs.append(
-            jnp.concatenate([ur * vr + ui * vi, ur * vi - ui * vr], 1).astype(BF16)
-        )
         both = inverse(leave[...], [conv, back]).astype(BF16)
         send3[:, 0, j] = both[:, :block].reshape(near, far, block)
         send3[:, 1, j] = both[:, block:].reshape(near, far, block)
     recv3[h] = send3[h]
     send_all(near_peer, near, lambda t: send3.at[t], recv3, h, 3)
 
-    wait_blocks(sdp_recv, n_dp, recv_sem.at[2])
-    total = sdp_recv[0]
-    for i in range(1, n_dp):
-        total = total + sdp_recv[i]
-    total = jnp.sum(total, axis=1, keepdims=True) * (1.0 / math.sqrt(n_dp * ctx * block))
-    channel = lax.broadcasted_iota(jnp.int32, (2, 128), 0) * 128 + lax.broadcasted_iota(
-        jnp.int32, (2, 128), 1
-    )
-    zero = jnp.zeros((2, 128), F32)
-    s3[...] = jnp.where(channel == 2 * c, total[0:1], zero) + jnp.where(
-        channel == 2 * c + 1, total[1:2], zero
-    )
-    s3_recv[h] = s3[...]
-    send_all(near_peer, near, lambda t: s3, s3_recv, h, 4)
-
-    term = inverse(leave_nat[...], filter_specs).astype(BF16)
-    fsend[:, 0] = term[:, :block].reshape(n_dp, ctx // n_dp, block)
-    fsend[:, 1] = term[:, block:].reshape(n_dp, ctx // n_dp, block)
-    frecv[d] = fsend[d]
-    send_all(dp_peer, n_dp, lambda t: fsend.at[t], frecv, d, 5)
-
-    wait_blocks(recv3, near, recv_sem.at[3])
+    wait_blocks(far_recv, far, recv_sem, 7)
+    dp_sum[...] = total(far_recv, far)
+    dp_recv[d] = dp_sum[...]
+    send_all(dp_peer, n_dp, lambda t: dp_sum, dp_recv, d, 2)
+
+    wait_blocks(recv3, near, recv_sem, 3)
     rows = jnp.concatenate(
         [recv3[:, 0].reshape(chans, block), recv3[:, 1].reshape(chans, block)], 1
     )
@@ -267,21 +284,7 @@
     recv4[g] = send4[g]
     send_all(far_peer, far, lambda t: send4.at[t], recv4, g, 6)
 
-    wait_blocks(s3_recv, near, recv_sem.at[4])
-    total = s3_recv[0]
-    for i in range(1, near):
-        total = total + s3_recv[i]
-    s4[...] = total
-    s4_recv[g] = total
-    send_all(far_peer, far, lambda t: s4, s4_recv, g, 7)
-
-    wait_blocks(frecv, n_dp, recv_sem.at[5])
-    grad = frecv[0].astype(F32)
-    for i in range(1, n_dp):
-        grad = grad + frecv[i].astype(F32)
-    filter_ref[...] = grad * (1.0 / math.sqrt(n_dp * ctx * block))
-
-    wait_blocks(recv4, far, recv_sem.at[6])
+    wait_blocks(recv4, far, recv_sem, 6)
     tokens = flip(
         jnp.concatenate(
             [recv4[:, 0].reshape(chans, block), recv4[:, 1].reshape(chans, block)], 1
@@ -290,20 +293,23 @@
     conv_ref[...] = tokens[:block]
     back_ref[...] = tokens[block:]
 
-    wait_blocks(s4_recv, far, recv_sem.at[7])
-    total = s4_recv[0]
-    for i in range(1, far):
-        total = total + s4_recv[i]
-    skip_ref[...] = total
-
-    wait_blocks(recv1, far, send_sem.at[0])
-    wait_blocks(recv2, near, send_sem.at[1])
-    wait_blocks(sdp_recv, n_dp, send_sem.at[2])
-    wait_blocks(recv3, near, send_sem.at[3])
-    wait_blocks(s3_recv, near, send_sem.at[4])
-    wait_blocks(frecv, n_dp, send_sem.at[5])
-    wait_blocks(recv4, far, send_sem.at[6])
-    wait_blocks(s4_recv, far, send_sem.at[7])
+    scale = 1.0 / math.sqrt(n_dp * ctx * block)
+    wait_blocks(dp_recv, n_dp, recv_sem, 2)
+    skip_ref[...] = total(dp_recv, n_dp) * scale
+    wait_blocks(frecv, n_dp, recv_sem, 5)
+    grad = frecv[0].astype(F32)
+    for i in range(1, n_dp):
+        grad = grad + frecv[i].astype(F32)
+    filter_ref[...] = grad * scale
+
+    wait_blocks(recv1, far, send_sem, 0)
+    wait_blocks(recv2, near, send_sem, 1)
+    wait_blocks(dp_recv, n_dp, send_sem, 2)
+    wait_blocks(recv3, near, send_sem, 3)
+    wait_blocks(near_recv, near, send_sem, 4)
+    wait_blocks(frecv, n_dp, send_sem, 5)
+    wait_blocks(recv4, far, send_sem, 6)
+    wait_blocks(far_recv, far, send_sem, 7)
 
 
 def per_device(input_gate, values, output_gate, grad_out, filter_taps, skip_gain):
@@ -314,13 +320,13 @@
     rows = np.arange(ctx).reshape(far, near).T.reshape(-1)
     tables = dft_tables(ctx, block, rows, 1.0 / (2 * ctx * block))
     gates = (input_gate[0], values[0], output_gate[0], grad_out[0])
-    operands = gates + (filter_taps.reshape(-1, ctx, block),) + tables
+    operands = gates + (filter_taps,) + tables
     share = ctx // n_dp
     outs = (
         jax.ShapeDtypeStruct((block, chans), BF16),
         jax.ShapeDtypeStruct((block, chans), BF16),
         jax.ShapeDtypeStruct((2, share, block), F32),
-        jax.ShapeDtypeStruct((2, 128), F32),
+        jax.ShapeDtypeStruct((1, chans), F32),
     )
     vmem = pltpu.VMEM
     conv_out, conv_back, filter_grad, skip_grad = pl.pallas_call(
@@ -329,13 +335,15 @@
         in_specs=[pl.BlockSpec(memory_space=pl.ANY)] * len(operands),
         out_specs=tuple(pl.BlockSpec(memory_space=pltpu.VMEM) for _ in outs),
         scratch_shapes=[vmem(x.shape, x.dtype) for x in operands]
+        + [vmem((2, ctx, block), F32)]
+        + [vmem(tables[i].shape, BF16) for i in (0, 3, 4, 5, 6, 7)]
         + [vmem((far, 2, 2 * near, block), BF16)] * 2
         + [vmem((near, 2, 2, far, block), BF16)] * 4
         + [vmem((far, 2, 2 * near, block), BF16)] * 2
         + [vmem((n_dp, 2, share, block), BF16)] * 2
-        + [vmem((2, block), F32), vmem((n_dp, 2, block), F32)]
-        + [vmem((2, 128), F32), vmem((near, 2, 128), F32)]
-        + [vmem((2, 128), F32), vmem((far, 2, 128), F32)]
+        + [vmem((1, chans), F32), vmem((near, 1, chans), F32)]
+        + [vmem((1, chans), F32), vmem((far, 1, chans), F32)]
+        + [vmem((1, chans), F32), vmem((n_dp, 1, chans), F32)]
         + [vmem((2, 2 * ctx, 2 * block), F32)]
         + [
             pltpu.SemaphoreType.DMA((len(operands),)),
@@ -343,7 +351,7 @@
             pltpu.SemaphoreType.DMA((8,)),
         ],
         compiler_params=pltpu.CompilerParams(
-            collective_id=0, has_side_effects=True, vmem_limit_bytes=48 * 1024 * 1024
+            collective_id=0, has_side_effects=True, vmem_limit_bytes=64 * 1024 * 1024
         ),
         name="mixer",
     )(*operands)
@@ -360,7 +368,7 @@
         grad_value[None],
         grad_output[None],
         filter_grad.reshape(2, share * block),
-        skip_grad.reshape(-1)[:chans],
+        skip_grad.reshape(-1),
     )
 
 

time: 57.5 us -> 45.8 us (0.80); the launches traced: 56.4 us -> 45.5 us
  local copies, waits for them, and re-layouts: 11.7 us -> 3.31 us
  Pallas kernels: 43.3 us -> 39.9 us
  other arithmetic: 0.74 us -> 1.71 us
    unnamed x29 -> x8, local copies, waits for them, and re-layouts: 11.7 us -> 3.31 us
    pallas_call x1, Pallas kernels: 43.3 us -> 39.9 us  [per_device(): pl.pallas_call(functools.partial(mixer_kernel, (n_dp, far, near, chans, b...]
    broadcast_in_dim x1, other arithmetic: 0.74 us -> 1.71 us  [per_device(): grad_value[None]]
where the time goes in v2:
time: 45.8 us; the launch traced here: 45.5 us
  Pallas kernels  39.9 us (87%)
  local copies, waits for them, and re-layouts  3.31 us (7%)
  other arithmetic  1.71 us (4%)
  between operations  0.65 us (1%)
    pallas_call x1, Pallas kernels, per_device(): pl.pallas_call(functools.partial(mixer_kernel, (n_dp, far, near, chans, b...  39.9 us
    unnamed x8, local copies, waits for them, and re-layouts  3.31 us
    broadcast_in_dim x1, other arithmetic, per_device(): grad_value[None]  1.71 us

profile of v2, /device:TPU:1, one launch (start us, length us, event | category | flops | bytes accessed | tf_op | source)
XLA Modules:
  0.0 45.5 jit_solution(5658797808599573245)
XLA Ops:
  0.6 39.9 %mixer.1 = (bf16[128,256]{1,0:T(8,128)(2,1)}, bf16[128,256]{1,0:T(8,128)(2,1)}, f32[2,32,128]{2,1,0:T(8,128)}, f32[1,256]{1,0:T(1,128)}) custom-call(bf16[128,256]{1,0:T(8,128)(2,1)} %bitcast.24, bf16[128,256]{1,0:T(8,128)(2,1)} %bitcast.25, bf16[128,256]{1,0:T(8,128)(2,1)} %bitcast.26, bf16[128,256]{1,0:T(8,128)(2,1)} %bitcast.27, ...), custom_call_target="tpu_custom_call" | custom-call | tf_op jit(solution)/shard_map/mixer/pallas_call | solution.py:332
  40.5 0.0 copy-start
  40.5 1.4 %copy.21 = f32[1,2,32,128]{3,1,2,0:T(2,128)} copy(f32[1,2,32,128]{3,2,1,0:T(8,128)} %bitcast.29) | data formatting | bytes 65536
  41.9 0.0 copy-start.1
  41.9 0.0 copy-done
  41.9 0.7 %copy-done.1 = f32[256]{0:T(256)S(1)} copy-done((f32[256]{0:T(256)S(1)}, f32[256]{0:T(256)}, u32[]{:S(2)}) %copy-start.1) | copy-done | bytes 1048
  42.6 1.7 %fusion.5 = (bf16[1,128,256]{2,1,0:T(8,128)(2,1)}, bf16[1,128,256]{2,1,0:T(8,128)(2,1)}, bf16[1,128,256]{2,1,0:T(8,128)(2,1)}) fusion(bf16[128,256]{1,0:T(8,128)(2,1)} %get-tuple-element.9, f32[256]{0:T(256)S(1)} %copy-done.1, bf16[1,128,256]{2,1,0:T(8,128)(2,1)} %param.17, bf16[1,128,256]{2,1,0:T(8,128)(2,1)} %param.16, ...), kind=kLoop, calls=%fused_computation.11 | loop fusion | flops 720896 | bytes 590848 | tf_op jit(solution)/shard_map/broadcast_in_dim | solution.py:368
  44.3 0.0 copy-start.2
  44.3 0.6 %copy-done.2 = f32[1,256]{1,0:T(1,128)S(1)} copy-done((f32[1,256]{1,0:T(1,128)S(1)}, f32[1,256]{1,0:T(1,128)}, u32[]{:S(2)}) %copy-start.2) | copy-done | bytes 1048
  45.0 0.6 %copy.23 = f32[256]{0:T(256)} copy(f32[256]{0:T(256)S(1)} %bitcast.30) | data formatting | bytes 2048
Async XLA Ops:
  40.5 1.4 %copy-start = (bf16[1,128,256]{2,1,0:T(8,128)(2,1)S(1)}, bf16[1,128,256]{2,1,0:T(8,128)(2,1)}, u32[]{:S(2)}) copy-start(bf16[1,128,256]{2,1,0:T(8,128)(2,1)} %param.14) | copy-start | bytes 196612
  41.9 0.7 %copy-start.1 = (f32[256]{0:T(256)S(1)}, f32[256]{0:T(256)}, u32[]{:S(2)}) copy-start(f32[256]{0:T(256)} %param.19) | copy-start | bytes 3076
  44.3 0.6 %copy-start.2 = (f32[1,256]{1,0:T(1,128)S(1)}, f32[1,256]{1,0:T(1,128)}, u32[]{:S(2)}) copy-start(f32[1,256]{1,0:T(1,128)} %get-tuple-element.12) | copy-start | bytes 3076

commit v3 on v2

v3 whole, which is shorter than its diff:
```python
import functools
import math

import jax
import jax.numpy as jnp
import numpy as np
from jax import lax
from jax.experimental import pallas as pl
from jax.experimental.pallas import tpu as pltpu
from jax.sharding import PartitionSpec as P

MESH = pl.DeviceIdType.MESH
F32 = jnp.float32
BF16 = jnp.bfloat16


def group_sizes(context):
    near = 1
    while 2 * near * near * 2 <= context:
        near *= 2
    return context // near, near


def dft_tables(pieces, block_len, rows, scale):
    outer = 2 * pieces
    total = outer * block_len

    def angle(first, second, modulus):
        return (first[:, None] * second[None, :] % modulus) * (2.0 * math.pi / modulus)

    across = np.arange(pieces)
    outer_index = np.arange(outer)
    inner_index = np.arange(block_len)
    first = angle(outer_index, across, outer)
    entry = np.concatenate([np.cos(first), -np.sin(first)], 0)
    twist = angle(outer_index, inner_index, total)
    twist_cos, twist_sin = np.cos(twist), np.sin(twist)
    inner = angle(inner_index, inner_index, block_len)
    cosine, sine = np.cos(inner), np.sin(inner)
    forward_inner = np.block([[cosine, -sine], [sine, cosine]])
    inverse_inner = np.block([[cosine, sine], [-sine, cosine]])
    last = angle(across, outer_index, outer)
    leave = np.concatenate([np.cos(last), -np.sin(last)], 1) * scale

    def low(table):
        return table.astype(BF16).astype(np.float32)

    return (
        low(entry),
        twist_cos.astype(np.float32),
        twist_sin.astype(np.float32),
        low(forward_inner),
        low(entry[:, rows]),
        low(inverse_inner),
        low(leave[rows]),
        low(leave),
    )


def dot(a, b):
    return jnp.dot(a, b, preferred_element_type=F32)


def flip(x):
    n = x.shape[1]
    eye = (
        lax.broadcasted_iota(jnp.int32, (n, n), 0) == lax.broadcasted_iota(jnp.int32, (n, n), 1)
    ).astype(BF16)
    return lax.dot_general(
        eye, x, (((1,), (1,)), ((), ())), preferred_element_type=F32
    ).astype(BF16)


def regroup(x, outer, inner):
    n = outer * inner
    row = lax.broadcasted_iota(jnp.int32, (n, n), 0)
    col = lax.broadcasted_iota(jnp.int32, (n, n), 1)
    place = (col == (row % outer) * inner + row // outer).astype(BF16)
    return dot(place, x).astype(BF16)


def mixer_kernel(
    sizes,
    ig_hbm, va_hbm, og_hbm, go_hbm, gain_hbm, taps_hbm, entry_nat_hbm, cos_hbm, sin_hbm, fwd_hbm,
    entry_hbm, inv_hbm, leave_hbm, leave_nat_hbm,
    gin_hbm, gval_hbm, gout_hbm, filter_hbm, skip_hbm,
    ig, va, og, go, gain, taps, entry_nat_in, cos, sin, fwd_in, entry_in, inv_in, leave_in,
    leave_nat_in, taps_rows, entry_nat, fwd, entry, inv, leave, leave_nat,
    gin, gval, gout, filter_out, skip_out,
    send1, recv1, send2, recv2, send3, recv3, send4, recv4,
    near_sum, near_recv, far_sum, far_recv, fsend, frecv, dp_sum, dp_recv, kern,
    load_sem, store_sem, send_sem, recv_sem, fsend_sem, frecv_sem, dsend_sem, drecv_sem,
):
    n_dp, far, near, chans, block = sizes
    ctx = far * near
    outer = 2 * ctx
    d = lax.axis_index("dp")
    c = lax.axis_index("context")
    g = c // near
    h = c % near

    pairs = (
        (ig_hbm, ig), (va_hbm, va), (og_hbm, og), (go_hbm, go), (taps_hbm, taps),
        (entry_nat_hbm, entry_nat_in), (cos_hbm, cos), (sin_hbm, sin), (fwd_hbm, fwd_in),
        (entry_hbm, entry_in), (inv_hbm, inv_in), (leave_hbm, leave_in),
        (leave_nat_hbm, leave_nat_in), (gain_hbm, gain),
    )
    loads = [pltpu.make_async_copy(src, dst, load_sem.at[i]) for i, (src, dst) in enumerate(pairs)]
    for load in loads[:4]:
        load.start()

    def far_peer(i):
        t = lax.rem(g + i, far)
        return t, (d, t * near + h)

    def near_peer(i):
        t = lax.rem(h + i, near)
        return t, (d, g * near + t)

    barrier = pltpu.get_barrier_semaphore()

    def greet(peer):
        def step(i, carry):
            pl.semaphore_signal(barrier, inc=1, device_id=peer(i)[1], device_id_type=MESH)
            return carry

        return step

    half = n_dp // 2

    def order(t):
        return t + (t // half) * (half - 1 - 2 * lax.rem(t, half))

    ahead = order(d)
    others = [lax.rem(d + i, n_dp) for i in range(1, n_dp)]
    lax.fori_loop(1, far, greet(far_peer), 0)
    lax.fori_loop(1, near, greet(near_peer), 0)
    for t in others:

        @pl.when(order(t) > ahead)
        def _():
            pl.semaphore_signal(barrier, inc=1, device_id=(t, c), device_id_type=MESH)

    for load in loads[4:]:
        load.start()

    def send_all(peer, count, src, dst, own, sem):
        def step(i, carry):
            t, target = peer(i)
            pltpu.make_async_remote_copy(
                src_ref=src(t),
                dst_ref=dst.at[own],
                send_sem=send_sem.at[sem],
                recv_sem=recv_sem.at[sem],
                device_id=target,
                device_id_type=MESH,
            ).start()
            return carry

        lax.fori_loop(1, count, step, 0)

    def wait_blocks(dst, count, sems, i):
        part = dst.at[pl.ds(0, count - 1)]
        pltpu.make_async_copy(part, part, sems.at[i]).wait()

    def wait_one(ref, sem):
        pltpu.make_async_copy(ref, ref, sem).wait()

    def total(blocks, count):
        value = blocks[0]
        for i in range(1, count):
            value = value + blocks[i]
        return value

    def product(a, b):
        return (a[...].astype(F32) * b[...].astype(F32)).astype(BF16)

    for i in range(4):
        loads[i].wait()
    mixed, gmix = product(ig, va), product(go, og)
    for i, tokens in enumerate((mixed, gmix)):
        send1[i] = flip(tokens).reshape(far, 2 * near, block)
        recv1[i, g] = send1[i, g]
    near_sum[...] = jnp.sum(mixed.astype(F32) * gmix.astype(F32), axis=0, keepdims=True)
    near_recv[h] = near_sum[...]

    pl.semaphore_wait(barrier, far + near - 2 + ahead)
    for i in range(2):
        send_all(far_peer, far, lambda t: send1.at[i, t], recv1.at[i], g, i)
    send_all(near_peer, near, lambda t: near_sum, near_recv, h, 8)

    def forward(table, x):
        section = dot(table, x)
        out = []
        for i in range(x.shape[1] // block):
            re = section[:outer, i * block : (i + 1) * block]
            im = section[outer:, i * block : (i + 1) * block]
            turned = jnp.concatenate(
                [
                    (re * cos[...] + im * sin[...]).astype(BF16),
                    (im * cos[...] - re * sin[...]).astype(BF16),
                ],
                1,
            )
            out.append(dot(turned, fwd[...]))
        return out

    def inverse(table, spectra):
        real, imag = [], []
        for spectrum in spectra:
            back = dot(spectrum, inv[...])
            re, im = back[:, :block], back[:, block:]
            real.append((re * cos[...] - im * sin[...]).astype(BF16))
            imag.append((im * cos[...] + re * sin[...]).astype(BF16))
        turned = jnp.concatenate([jnp.concatenate(real, 1), jnp.concatenate(imag, 1)], 0)
        return dot(table, turned).astype(BF16)

    for i in range(4, 14):
        loads[i].wait()
    entry_nat[...] = entry_nat_in[...].astype(BF16)
    fwd[...] = fwd_in[...].astype(BF16)
    for j in range(2):
        for a in range(ctx):
            taps_rows[j, pl.ds(a, 1)] = taps[pl.ds(j, 1), pl.ds(a * block, block)].astype(F32)
    both = jnp.concatenate([taps_rows[0], taps_rows[1]], 1).astype(BF16)
    for j, spectrum in enumerate(forward(entry_nat[...], both)):
        kern[j] = spectrum
    entry[...] = entry_in[...].astype(BF16)
    inv[...] = inv_in[...].astype(BF16)
    leave[...] = leave_in[...].astype(BF16)
    leave_nat[...] = leave_nat_in[...].astype(BF16)

    for i in range(2):
        wait_blocks(recv1.at[i], far, recv_sem, i)
        rows = regroup(recv1[i].reshape(chans, block), far, 2 * near)
        send2[i] = rows.reshape(near, 2, far, block)
        recv2[i, h] = send2[i, h]
        send_all(near_peer, near, lambda t: send2.at[i, t], recv2.at[i], h, 2 + i)

    wait_blocks(near_recv, near, recv_sem, 8)
    far_sum[...] = total(near_recv, near)
    far_recv[g] = far_sum[...]
    send_all(far_peer, far, lambda t: far_sum, far_recv, g, 9)

    spectra = []
    for i in range(2):
        wait_blocks(recv2.at[i], near, recv_sem, 2 + i)
        both = jnp.concatenate([recv2[i, :, j].reshape(ctx, block) for j in range(2)], 1)
        spectra.append([(s[:, :block], s[:, block:]) for s in forward(entry[...], both)])
    sources, gradients = spectra

    specs = []
    for (ur, ui), (vr, vi) in zip(sources, gradients):
        specs.append(jnp.concatenate([ur * vr + ui * vi, ur * vi - ui * vr], 1).astype(BF16))
    term = inverse(leave_nat[...], specs)
    for j in range(2):
        part = term[:, j * block : (j + 1) * block]
        fsend[:, j] = part.reshape(n_dp, ctx // n_dp, block)
    frecv[d] = fsend[d]
    wait_blocks(far_recv, far, recv_sem, 9)
    dp_sum[...] = total(far_recv, far)
    dp_recv[d] = dp_sum[...]

    def send_shares(t):
        for src, dst, out, come in (
            (fsend.at[t], frecv.at[d], fsend_sem.at[t], frecv_sem.at[d]),
            (dp_sum, dp_recv.at[d], dsend_sem.at[t], drecv_sem.at[d]),
        ):
            pltpu.make_async_remote_copy(
                src_ref=src,
                dst_ref=dst,
                send_sem=out,
                recv_sem=come,
                device_id=(t, c),
                device_id_type=MESH,
            ).start()

    for t in others:

        @pl.when(order(t) < ahead)
        def _():
            send_shares(t)

    kernels = [(kern[j][:, :block], kern[j][:, block:]) for j in range(2)]
    convs, backs = [], []
    for (ur, ui), (vr, vi), (kr, ki) in zip(sources, gradients, kernels):
        convs.append(jnp.concatenate([ur * kr - ui * ki, ur * ki + ui * kr], 1).astype(BF16))
        backs.append(jnp.concatenate([kr * vr + ki * vi, kr * vi - ki * vr], 1).astype(BF16))
    for i, specs in enumerate((convs, backs)):
        both = inverse(leave[...], specs)
        for j in range(2):
            part = both[:, j * block : (j + 1) * block]
            send3[i, :, j] = part.reshape(near, far, block)
        recv3[i, h] = send3[i, h]
        send_all(near_peer, near, lambda t: send3.at[i, t], recv3.at[i], h, 4 + i)

    for i in range(2):
        wait_blocks(recv3.at[i], near, recv_sem, 4 + i)
        rows = regroup(recv3[i].reshape(chans, block), 2 * near, far)
        send4[i] = rows.reshape(far, 2 * near, block)
        recv4[i, g] = send4[i, g]
        send_all(far_peer, far, lambda t: send4.at[i, t], recv4.at[i], g, 6 + i)

    stores = [
        pltpu.make_async_copy(src, dst, store_sem.at[i])
        for i, (src, dst) in enumerate(
            (
                (gout, gout_hbm), (gin, gin_hbm), (gval, gval_hbm),
                (skip_out, skip_hbm), (filter_out, filter_hbm),
            )
        )
    ]
    wait_blocks(recv4.at[0], far, recv_sem, 6)
    conv = flip(recv4[0].reshape(chans, block)).astype(F32)
    gains = gain[...]
    gout[...] = (
        go[...].astype(F32) * (conv + gains * product(ig, va).astype(F32))
    ).astype(BF16)
    stores[0].start()
    wait_blocks(recv4.at[1], far, recv_sem, 7)
    back = flip(recv4[1].reshape(chans, block)).astype(F32)
    grad_mixed = back + gains * product(go, og).astype(F32)
    gin[...] = (grad_mixed * va[...].astype(F32)).astype(BF16)
    gval[...] = (grad_mixed * ig[...].astype(F32)).astype(BF16)
    stores[1].start()
    stores[2].start()

    for t in others:

        @pl.when(order(t) > ahead)
        def _():
            wait_one(frecv.at[t], frecv_sem.at[t])
            send_shares(t)

    for t in others:

        @pl.when(order(t) < ahead)
        def _():
            wait_one(frecv.at[t], frecv_sem.at[t])

    scale = 1.0 / math.sqrt(n_dp * ctx * block)
    grad = frecv[0].astype(F32)
    for i in range(1, n_dp):
        grad = grad + frecv[i].astype(F32)
    grad = grad * scale
    for j in range(2):
        for a in range(ctx // n_dp):
            filter_out[pl.ds(j, 1), pl.ds(a * block, block)] = grad[j, a : a + 1]
    stores[4].start()
    for t in others:
        wait_one(dp_recv.at[t], drecv_sem.at[t])
    skip_out[...] = total(dp_recv, n_dp) * scale
    stores[3].start()

    for i in range(2):
        wait_blocks(recv1.at[i], far, send_sem, i)
        wait_blocks(recv2.at[i], near, send_sem, 2 + i)
        wait_blocks(recv3.at[i], near, send_sem, 4 + i)
        wait_blocks(recv4.at[i], far, send_sem, 6 + i)
    wait_blocks(near_recv, near, send_sem, 8)
    wait_blocks(far_recv, far, send_sem, 9)
    for t in others:
        wait_one(fsend.at[t], fsend_sem.at[t])
        wait_one(dp_sum, dsend_sem.at[t])
    for store in stores:
        store.wait()


def copy_kernel(*refs):
    n = (len(refs) - 1) // 2
    copies = [pltpu.make_async_copy(refs[i], refs[n + i], refs[-1].at[i]) for i in range(n)]
    for copy in copies:
        copy.start()
    for copy in copies:
        copy.wait()


def per_device(input_gate, values, output_gate, grad_out, filter_taps, skip_gain):
    n_dp = lax.axis_size("dp")
    ctx = lax.axis_size("context")
    far, near = group_sizes(ctx)
    block, chans = input_gate.shape[1:]
    rows = np.arange(ctx).reshape(far, near).T.reshape(-1)
    tables = dft_tables(ctx, block, rows, 1.0 / (2 * ctx * block))
    gates = (input_gate[0], values[0], output_gate[0], grad_out[0], skip_gain.reshape(1, -1))
    operands = gates + (filter_taps,) + tables
    share = ctx // n_dp
    outs = tuple(jax.ShapeDtypeStruct((block, chans), BF16) for _ in range(3)) + (
        jax.ShapeDtypeStruct((2, share * block), F32),
        jax.ShapeDtypeStruct((1, chans), F32),
    )
    vmem = pltpu.VMEM
    dma = pltpu.SemaphoreType.DMA
    results = pl.pallas_call(
        functools.partial(mixer_kernel, (n_dp, far, near, chans, block)),
        out_shape=outs,
        in_specs=[pl.BlockSpec(memory_space=pl.ANY)] * len(operands),
        out_specs=tuple(pl.BlockSpec(memory_space=pl.ANY) for _ in outs),
        scratch_shapes=[vmem(x.shape, x.dtype) for x in operands]
        + [vmem((2, ctx, block), F32)]
        + [vmem(tables[i].shape, BF16) for i in (0, 3, 4, 5, 6, 7)]
        + [vmem(x.shape, x.dtype) for x in outs]
        + [vmem((2, far, 2 * near, block), BF16)] * 2
        + [vmem((2, near, 2, far, block), BF16)] * 4
        + [vmem((2, far, 2 * near, block), BF16)] * 2
        + [vmem((1, chans), F32), vmem((near, 1, chans), F32)]
        + [vmem((1, chans), F32), vmem((far, 1, chans), F32)]
        + [vmem((n_dp, 2, share, block), BF16)] * 2
        + [vmem((1, chans), F32), vmem((n_dp, 1, chans), F32)]
        + [vmem((2, 2 * ctx, 2 * block), F32)]
        + [dma((len(operands),)), dma((len(outs),)), dma((10,)), dma((10,))]
        + [dma((n_dp,))] * 4,
        compiler_params=pltpu.CompilerParams(
            collective_id=0, has_side_effects=True, vmem_limit_bytes=64 * 1024 * 1024
        ),
        name="mixer",
    )(*operands)
    grad_input, grad_value, grad_output, filter_grad, skip_grad = pl.pallas_call(
        copy_kernel,
        out_shape=outs,
        in_specs=[pl.BlockSpec(memory_space=pl.ANY)] * len(outs),
        out_specs=tuple(pl.BlockSpec(memory_space=pl.ANY) for _ in outs),
        scratch_shapes=[dma((len(outs),))],
        compiler_params=pltpu.CompilerParams(vmem_limit_bytes=64 * 1024 * 1024),
        name="results",
    )(*results)
    return (
        grad_input[None],
        grad_value[None],
        grad_output[None],
        filter_grad,
        skip_grad.reshape(-1),
    )


def solution(mesh):
    return jax.shard_map(
        per_device,
        mesh=mesh,
        in_specs=(
            P("dp", "context", None),
            P("dp", "context", None),
            P("dp", "context", None),
            P("dp", "context", None),
            P("context", None),
            P(),
        ),
        out_specs=(
            P("dp", "context", None),
            P("dp", "context", None),
            P("dp", "context", None),
            P("context", "dp"),
            P(),
        ),
        check_vma=False,
    )
```

time: 45.8 us -> 44.4 us (0.969)
  the two profiles are of different devices: /device:TPU:1 before, /device:TPU:448 now
where the time goes in v3:
time: 44.4 us; the launch traced here: 44.2 us
  Pallas kernels  43.6 us (98%)
  between operations  0.64 us (1%)
    pallas_call x1, Pallas kernels, per_device(): pl.pallas_call(functools.partial(mixer_kernel, (n_dp, far, near, chans, b...  35.5 us
    pallas_call x1, Pallas kernels, per_device(): pl.pallas_call(copy_kernel, out_shape=outs, in_specs=[pl.BlockSpec(memory...  8.13 us

profile of v3, /device:TPU:448, one launch (start us, length us, event | category | flops | bytes accessed | tf_op | source)
XLA Modules:
  0.0 44.2 jit_solution(805742548712818478)
XLA Ops:
  0.6 35.5 %mixer.1 = (bf16[128,256]{1,0:T(8,128)(2,1)}, bf16[128,256]{1,0:T(8,128)(2,1)}, bf16[128,256]{1,0:T(8,128)(2,1)}, f32[2,4096]{1,0:T(2,128)}, f32[1,256]{1,0:T(1,128)}) custom-call(bf16[128,256]{1,0:T(8,128)(2,1)} %bitcast.9, bf16[128,256]{1,0:T(8,128)(2,1)} %bitcast.10, bf16[128,256]{1,0:T(8,128)(2,1)} %bitcast.11, bf16[128,256]{1,0:T(8,128)(2,1)} %bitcast.12, ...), custom_call_target="tpu_custom_call" | custom-call | tf_op jit(solution)/shard_map/mixer/pallas_call | solution.py:394
  36.1 8.1 %results.1 = (bf16[128,256]{1,0:T(8,128)(2,1)}, bf16[128,256]{1,0:T(8,128)(2,1)}, bf16[128,256]{1,0:T(8,128)(2,1)}, f32[2,4096]{1,0:T(2,128)}, f32[1,256]{1,0:T(1,128)}) custom-call(bf16[128,256]{1,0:T(8,128)(2,1)} %get-tuple-element.15.refs_0_, bf16[128,256]{1,0:T(8,128)(2,1)} %get-tuple-element.16.refs_1_, bf16[128,256]{1,0:T(8,128)(2,1)} %get-tuple-element.17.refs_2_, ...), custom_call_target="tpu_custom_call" | custom-call | tf_op jit(solution)/shard_map/results/pallas_call | solution.py:418

commit v4 on v3

--- a/solution.py
+++ b/solution.py
@@ -88,8 +88,9 @@
     leave_nat_in, taps_rows, entry_nat, fwd, entry, inv, leave, leave_nat,
     gin, gval, gout, filter_out, skip_out,
     send1, recv1, send2, recv2, send3, recv3, send4, recv4,
-    near_sum, near_recv, far_sum, far_recv, fsend, frecv, dp_sum, dp_recv, kern,
+    near_sum, near_recv, far_sum, far_recv, fsend, frecv, dp_sum, dp_recv, word, words, kern,
     load_sem, store_sem, send_sem, recv_sem, fsend_sem, frecv_sem, dsend_sem, drecv_sem,
+    wsend_sem, wrecv_sem,
 ):
     n_dp, far, near, chans, block = sizes
     ctx = far * near
@@ -132,7 +133,7 @@
         return t + (t // half) * (half - 1 - 2 * lax.rem(t, half))
 
     ahead = order(d)
-    others = [lax.rem(d + i, n_dp) for i in range(1, n_dp)]
+    others = [lax.rem(d + n_dp - i, n_dp) for i in (2, 1, 3)[: n_dp - 1]] if n_dp > 2 else [1 - d]
     lax.fori_loop(1, far, greet(far_peer), 0)
     lax.fori_loop(1, near, greet(near_peer), 0)
     for t in others:
@@ -183,11 +184,24 @@
         recv1[i, g] = send1[i, g]
     near_sum[...] = jnp.sum(mixed.astype(F32) * gmix.astype(F32), axis=0, keepdims=True)
     near_recv[h] = near_sum[...]
+    word[...] = jnp.zeros(word.shape, F32)
 
     pl.semaphore_wait(barrier, far + near - 2 + ahead)
     for i in range(2):
         send_all(far_peer, far, lambda t: send1.at[i, t], recv1.at[i], g, i)
     send_all(near_peer, near, lambda t: near_sum, near_recv, h, 8)
+    for t in others:
+
+        @pl.when(order(t) < ahead)
+        def _():
+            pltpu.make_async_remote_copy(
+                src_ref=word,
+                dst_ref=words.at[d],
+                send_sem=wsend_sem.at[t],
+                recv_sem=wrecv_sem.at[d],
+                device_id=(t, c),
+                device_id_type=MESH,
+            ).start()
 
     def forward(table, x):
         section = dot(table, x)
@@ -293,6 +307,13 @@
             send3[i, :, j] = part.reshape(near, far, block)
         recv3[i, h] = send3[i, h]
         send_all(near_peer, near, lambda t: send3.at[i, t], recv3.at[i], h, 4 + i)
+
+    for t in others:
+
+        @pl.when(order(t) > ahead)
+        def _():
+            wait_one(words.at[t], wrecv_sem.at[t])
+            send_shares(t)
 
     for i in range(2):
         wait_blocks(recv3.at[i], near, recv_sem, 4 + i)
@@ -326,18 +347,7 @@
     stores[2].start()
 
     for t in others:
-
-        @pl.when(order(t) > ahead)
-        def _():
-            wait_one(frecv.at[t], frecv_sem.at[t])
-            send_shares(t)
-
-    for t in others:
-
-        @pl.when(order(t) < ahead)
-        def _():
-            wait_one(frecv.at[t], frecv_sem.at[t])
-
+        wait_one(frecv.at[t], frecv_sem.at[t])
     scale = 1.0 / math.sqrt(n_dp * ctx * block)
     grad = frecv[0].astype(F32)
     for i in range(1, n_dp):
@@ -362,17 +372,28 @@
     for t in others:
         wait_one(fsend.at[t], fsend_sem.at[t])
         wait_one(dp_sum, dsend_sem.at[t])
+
+        @pl.when(order(t) < ahead)
+        def _():
+            wait_one(word, wsend_sem.at[t])
+
     for store in stores:
         store.wait()
 
 
 def copy_kernel(*refs):
-    n = (len(refs) - 1) // 2
-    copies = [pltpu.make_async_copy(refs[i], refs[n + i], refs[-1].at[i]) for i in range(n)]
-    for copy in copies:
-        copy.start()
-    for copy in copies:
-        copy.wait()
+    n = (len(refs) - 2) // 3
+    sources, targets, held = refs[:n], refs[n : 2 * n], refs[2 * n : 3 * n]
+    come, gone = refs[3 * n :]
+    loads = [pltpu.make_async_copy(sources[i], held[i], come.at[i]) for i in range(n)]
+    stores = [pltpu.make_async_copy(held[i], targets[i], gone.at[i]) for i in range(n)]
+    for load in loads:
+        load.start()
+    for load, store in zip(loads, stores):
+        load.wait()
+        store.start()
+    for store in stores:
+        store.wait()
 
 
 def per_device(input_gate, values, output_gate, grad_out, filter_taps, skip_gain):
@@ -407,9 +428,10 @@
         + [vmem((1, chans), F32), vmem((far, 1, chans), F32)]
         + [vmem((n_dp, 2, share, block), BF16)] * 2
         + [vmem((1, chans), F32), vmem((n_dp, 1, chans), F32)]
+        + [vmem((1, 128), F32), vmem((n_dp, 1, 128), F32)]
         + [vmem((2, 2 * ctx, 2 * block), F32)]
         + [dma((len(operands),)), dma((len(outs),)), dma((10,)), dma((10,))]
-        + [dma((n_dp,))] * 4,
+        + [dma((n_dp,))] * 6,
         compiler_params=pltpu.CompilerParams(
             collective_id=0, has_side_effects=True, vmem_limit_bytes=64 * 1024 * 1024
         ),
@@ -420,7 +442,7 @@
         out_shape=outs,
         in_specs=[pl.BlockSpec(memory_space=pl.ANY)] * len(outs),
         out_specs=tuple(pl.BlockSpec(memory_space=pl.ANY) for _ in outs),
-        scratch_shapes=[dma((len(outs),))],
+        scratch_shapes=[vmem(x.shape, x.dtype) for x in outs] + [dma((len(outs),))] * 2,
         compiler_params=pltpu.CompilerParams(vmem_limit_bytes=64 * 1024 * 1024),
         name="results",
     )(*results)

time: 44.4 us -> 36.7 us (0.83)
  the two profiles are of different devices: /device:TPU:448 before, /device:TPU:1 now
where the time goes in v4:
time: 36.7 us; the launch traced here: 36.5 us
  Pallas kernels  35.9 us (98%)
  between operations  0.64 us (2%)
    pallas_call x1, Pallas kernels, per_device(): pl.pallas_call(functools.partial(mixer_kernel, (n_dp, far, near, chans, b...  34.3 us
    pallas_call x1, Pallas kernels, per_device(): pl.pallas_call(copy_kernel, out_shape=outs, in_specs=[pl.BlockSpec(memory...  1.63 us

profile of v4, /device:TPU:1, one launch (start us, length us, event | category | flops | bytes accessed | tf_op | source)
XLA Modules:
  0.0 36.5 jit_solution(13858433715427060056)
XLA Ops:
  0.6 34.3 %mixer.1 = (bf16[128,256]{1,0:T(8,128)(2,1)}, bf16[128,256]{1,0:T(8,128)(2,1)}, bf16[128,256]{1,0:T(8,128)(2,1)}, f32[2,4096]{1,0:T(2,128)}, f32[1,256]{1,0:T(1,128)}) custom-call(bf16[128,256]{1,0:T(8,128)(2,1)} %bitcast.9, bf16[128,256]{1,0:T(8,128)(2,1)} %bitcast.10, bf16[128,256]{1,0:T(8,128)(2,1)} %bitcast.11, bf16[128,256]{1,0:T(8,128)(2,1)} %bitcast.12, ...), custom_call_target="tpu_custom_call" | custom-call | tf_op jit(solution)/shard_map/mixer/pallas_call | solution.py:415
  34.9 1.6 %results.1 = (bf16[128,256]{1,0:T(8,128)(2,1)}, bf16[128,256]{1,0:T(8,128)(2,1)}, bf16[128,256]{1,0:T(8,128)(2,1)}, f32[2,4096]{1,0:T(2,128)}, f32[1,256]{1,0:T(1,128)}) custom-call(bf16[128,256]{1,0:T(8,128)(2,1)} %get-tuple-element.15.refs_0_, bf16[128,256]{1,0:T(8,128)(2,1)} %get-tuple-element.16.refs_1_, bf16[128,256]{1,0:T(8,128)(2,1)} %get-tuple-element.17.refs_2_, ...), custom_call_target="tpu_custom_call" | custom-call | tf_op jit(solution)/shard_map/results/pallas_call | solution.py:440

commit v5 on v4

--- a/solution.py
+++ b/solution.py
@@ -83,13 +83,12 @@
     sizes,
     ig_hbm, va_hbm, og_hbm, go_hbm, gain_hbm, taps_hbm, entry_nat_hbm, cos_hbm, sin_hbm, fwd_hbm,
     entry_hbm, inv_hbm, leave_hbm, leave_nat_hbm,
-    gin_hbm, gval_hbm, gout_hbm, filter_hbm, skip_hbm,
+    gin, gval, gout, filter_out, skip_out,
     ig, va, og, go, gain, taps, entry_nat_in, cos, sin, fwd_in, entry_in, inv_in, leave_in,
     leave_nat_in, taps_rows, entry_nat, fwd, entry, inv, leave, leave_nat,
-    gin, gval, gout, filter_out, skip_out,
     send1, recv1, send2, recv2, send3, recv3, send4, recv4,
     near_sum, near_recv, far_sum, far_recv, fsend, frecv, dp_sum, dp_recv, word, words, kern,
-    load_sem, store_sem, send_sem, recv_sem, fsend_sem, frecv_sem, dsend_sem, drecv_sem,
+    load_sem, send_sem, recv_sem, fsend_sem, frecv_sem, dsend_sem, drecv_sem,
     wsend_sem, wrecv_sem,
 ):
     n_dp, far, near, chans, block = sizes
@@ -322,29 +321,17 @@
         recv4[i, g] = send4[i, g]
         send_all(far_peer, far, lambda t: send4.at[i, t], recv4.at[i], g, 6 + i)
 
-    stores = [
-        pltpu.make_async_copy(src, dst, store_sem.at[i])
-        for i, (src, dst) in enumerate(
-            (
-                (gout, gout_hbm), (gin, gin_hbm), (gval, gval_hbm),
-                (skip_out, skip_hbm), (filter_out, filter_hbm),
-            )
-        )
-    ]
     wait_blocks(recv4.at[0], far, recv_sem, 6)
     conv = flip(recv4[0].reshape(chans, block)).astype(F32)
     gains = gain[...]
     gout[...] = (
         go[...].astype(F32) * (conv + gains * product(ig, va).astype(F32))
     ).astype(BF16)
-    stores[0].start()
     wait_blocks(recv4.at[1], far, recv_sem, 7)
     back = flip(recv4[1].reshape(chans, block)).astype(F32)
     grad_mixed = back + gains * product(go, og).astype(F32)
     gin[...] = (grad_mixed * va[...].astype(F32)).astype(BF16)
     gval[...] = (grad_mixed * ig[...].astype(F32)).astype(BF16)
-    stores[1].start()
-    stores[2].start()
 
     for t in others:
         wait_one(frecv.at[t], frecv_sem.at[t])
@@ -356,11 +343,9 @@
     for j in range(2):
         for a in range(ctx // n_dp):
             filter_out[pl.ds(j, 1), pl.ds(a * block, block)] = grad[j, a : a + 1]
-    stores[4].start()
     for t in others:
         wait_one(dp_recv.at[t], drecv_sem.at[t])
     skip_out[...] = total(dp_recv, n_dp) * scale
-    stores[3].start()
 
     for i in range(2):
         wait_blocks(recv1.at[i], far, send_sem, i)
@@ -377,23 +362,14 @@
         def _():
             wait_one(word, wsend_sem.at[t])
 
-    for store in stores:
-        store.wait()
-
 
 def copy_kernel(*refs):
-    n = (len(refs) - 2) // 3
-    sources, targets, held = refs[:n], refs[n : 2 * n], refs[2 * n : 3 * n]
-    come, gone = refs[3 * n :]
-    loads = [pltpu.make_async_copy(sources[i], held[i], come.at[i]) for i in range(n)]
-    stores = [pltpu.make_async_copy(held[i], targets[i], gone.at[i]) for i in range(n)]
-    for load in loads:
-        load.start()
-    for load, store in zip(loads, stores):
-        load.wait()
-        store.start()
-    for store in stores:
-        store.wait()
+    n = (len(refs) - 1) // 2
+    copies = [pltpu.make_async_copy(refs[i], refs[n + i], refs[-1].at[i]) for i in range(n)]
+    for copy in copies:
+        copy.start()
+    for copy in copies:
+        copy.wait()
 
 
 def per_device(input_gate, values, output_gate, grad_out, filter_taps, skip_gain):
@@ -414,13 +390,12 @@
     dma = pltpu.SemaphoreType.DMA
     results = pl.pallas_call(
         functools.partial(mixer_kernel, (n_dp, far, near, chans, block)),
-        out_shape=outs,
-        in_specs=[pl.BlockSpec(memory_space=pl.ANY)] * len(operands),
-        out_specs=tuple(pl.BlockSpec(memory_space=pl.ANY) for _ in outs),
+        out_shape=tuple(pltpu.VMEM(x.shape, x.dtype) for x in outs),
+        in_specs=[pl.BlockSpec(memory_space=pltpu.HBM)] * len(operands),
+        out_specs=tuple(pl.BlockSpec(memory_space=pltpu.VMEM) for _ in outs),
         scratch_shapes=[vmem(x.shape, x.dtype) for x in operands]
         + [vmem((2, ctx, block), F32)]
         + [vmem(tables[i].shape, BF16) for i in (0, 3, 4, 5, 6, 7)]
-        + [vmem(x.shape, x.dtype) for x in outs]
         + [vmem((2, far, 2 * near, block), BF16)] * 2
         + [vmem((2, near, 2, far, block), BF16)] * 4
         + [vmem((2, far, 2 * near, block), BF16)] * 2
@@ -430,20 +405,20 @@
         + [vmem((1, chans), F32), vmem((n_dp, 1, chans), F32)]
         + [vmem((1, 128), F32), vmem((n_dp, 1, 128), F32)]
         + [vmem((2, 2 * ctx, 2 * block), F32)]
-        + [dma((len(operands),)), dma((len(outs),)), dma((10,)), dma((10,))]
+        + [dma((len(operands),)), dma((10,)), dma((10,))]
         + [dma((n_dp,))] * 6,
         compiler_params=pltpu.CompilerParams(
-            collective_id=0, has_side_effects=True, vmem_limit_bytes=64 * 1024 * 1024
+            collective_id=0, has_side_effects=True, vmem_limit_bytes=32 * 1024 * 1024
         ),
         name="mixer",
-    )(*operands)
+    )(*(pltpu.with_memory_space_constraint(x, pltpu.HBM) for x in operands))
     grad_input, grad_value, grad_output, filter_grad, skip_grad = pl.pallas_call(
         copy_kernel,
         out_shape=outs,
-        in_specs=[pl.BlockSpec(memory_space=pl.ANY)] * len(outs),
+        in_specs=[pl.BlockSpec(memory_space=pltpu.VMEM)] * len(outs),
         out_specs=tuple(pl.BlockSpec(memory_space=pl.ANY) for _ in outs),
-        scratch_shapes=[vmem(x.shape, x.dtype) for x in outs] + [dma((len(outs),))] * 2,
-        compiler_params=pltpu.CompilerParams(vmem_limit_bytes=64 * 1024 * 1024),
+        scratch_shapes=[dma((len(outs),))],
+        compiler_params=pltpu.CompilerParams(vmem_limit_bytes=32 * 1024 * 1024),
         name="results",
     )(*results)
     return (

time: 36.7 us -> 35.2 us (0.959)
  Pallas kernels: 35.9 us -> 34.4 us
    pallas_call x1, Pallas kernels: 1.63 us -> 0.73 us  [per_device(): pl.pallas_call(copy_kernel, out_shape=outs, in_specs=[pl.BlockSpec(memory...]
    pallas_call x1, Pallas kernels: 34.3 us -> 33.6 us  [per_device(): pl.pallas_call(functools.partial(mixer_kernel, (n_dp, far, near, chans, b...]
where the time goes in v5:
time: 35.2 us; the launch traced here: 35 us
  Pallas kernels  34.4 us (98%)
  between operations  0.64 us (2%)
    pallas_call x1, Pallas kernels, per_device(): pl.pallas_call(functools.partial(mixer_kernel, (n_dp, far, near, chans, b...  33.6 us
    pallas_call x1, Pallas kernels, per_device(): pl.pallas_call(copy_kernel, out_shape=outs, in_specs=[pl.BlockSpec(memory...  0.73 us

profile of v5, /device:TPU:1, one launch (start us, length us, event | category | flops | bytes accessed | tf_op | source)
XLA Modules:
  0.0 35.0 jit_solution(16445689449822297409)
XLA Ops:
  0.6 33.6 %mixer.1 = (bf16[128,256]{1,0:T(8,128)(2,1)S(1)}, bf16[128,256]{1,0:T(8,128)(2,1)S(1)}, bf16[128,256]{1,0:T(8,128)(2,1)S(1)}, f32[2,4096]{1,0:T(2,128)S(1)}, f32[1,256]{1,0:T(1,128)S(1)}) custom-call(bf16[128,256]{1,0:T(8,128)(2,1)} %bitcast.9, bf16[128,256]{1,0:T(8,128)(2,1)} %bitcast.10, bf16[128,256]{1,0:T(8,128)(2,1)} %bitcast.11, ...), custom_call_target="tpu_custom_call" | custom-call | tf_op jit(solution)/shard_map/mixer/pallas_call | solution.py:391
  34.3 0.7 %results.1 = (bf16[128,256]{1,0:T(8,128)(2,1)}, bf16[128,256]{1,0:T(8,128)(2,1)}, bf16[128,256]{1,0:T(8,128)(2,1)}, f32[2,4096]{1,0:T(2,128)}, f32[1,256]{1,0:T(1,128)}) custom-call(bf16[128,256]{1,0:T(8,128)(2,1)S(1)} %get-tuple-element.15.refs_0_, bf16[128,256]{1,0:T(8,128)(2,1)S(1)} %get-tuple-element.16.refs_1_, ...), custom_call_target="tpu_custom_call" | custom-call | tf_op jit(solution)/shard_map/results/pallas_call | solution.py:415

commit v6 on v5

--- a/solution.py
+++ b/solution.py
@@ -21,7 +21,7 @@
     return context // near, near
 
 
-def dft_tables(pieces, block_len, rows, scale):
+def dft_tables(pieces, block_len, scale):
     outer = 2 * pieces
     total = outer * block_len
 
@@ -50,9 +50,7 @@
         twist_cos.astype(np.float32),
         twist_sin.astype(np.float32),
         low(forward_inner),
-        low(entry[:, rows]),
         low(inverse_inner),
-        low(leave[rows]),
         low(leave),
     )
 
@@ -61,35 +59,27 @@
     return jnp.dot(a, b, preferred_element_type=F32)
 
 
-def flip(x):
-    n = x.shape[1]
-    eye = (
-        lax.broadcasted_iota(jnp.int32, (n, n), 0) == lax.broadcasted_iota(jnp.int32, (n, n), 1)
-    ).astype(BF16)
-    return lax.dot_general(
-        eye, x, (((1,), (1,)), ((), ())), preferred_element_type=F32
-    ).astype(BF16)
-
-
-def regroup(x, outer, inner):
-    n = outer * inner
+def dot_rows(a, b):
+    return lax.dot_general(a, b, (((1,), (1,)), ((), ())), preferred_element_type=F32)
+
+
+def selector(n, place):
     row = lax.broadcasted_iota(jnp.int32, (n, n), 0)
     col = lax.broadcasted_iota(jnp.int32, (n, n), 1)
-    place = (col == (row % outer) * inner + row // outer).astype(BF16)
-    return dot(place, x).astype(BF16)
+    return (col == place(row)).astype(BF16)
 
 
 def mixer_kernel(
     sizes,
-    ig_hbm, va_hbm, og_hbm, go_hbm, gain_hbm, taps_hbm, entry_nat_hbm, cos_hbm, sin_hbm, fwd_hbm,
-    entry_hbm, inv_hbm, leave_hbm, leave_nat_hbm,
+    ig_hbm, va_hbm, og_hbm, go_hbm, gain_hbm, taps_hbm, entry_hbm, cos_hbm, sin_hbm, fwd_hbm,
+    inv_hbm, leave_hbm,
     gin, gval, gout, filter_out, skip_out,
-    ig, va, og, go, gain, taps, entry_nat_in, cos, sin, fwd_in, entry_in, inv_in, leave_in,
-    leave_nat_in, taps_rows, entry_nat, fwd, entry, inv, leave, leave_nat,
-    send1, recv1, send2, recv2, send3, recv3, send4, recv4,
+    ig, va, og, go, gain, taps, entry_in, cos, sin, fwd_in, inv_in, leave_in,
+    taps_rows, entry, fwd, inv, leave, by_channel, by_piece, of_piece,
+    there_out, there_in, back_out, back_in,
     near_sum, near_recv, far_sum, far_recv, fsend, frecv, dp_sum, dp_recv, word, words, kern,
     load_sem, send_sem, recv_sem, fsend_sem, frecv_sem, dsend_sem, drecv_sem,
-    wsend_sem, wrecv_sem,
+    wsend_sem, wrecv_sem, ready,
 ):
     n_dp, far, near, chans, block = sizes
     ctx = far * near
@@ -101,9 +91,8 @@
 
     pairs = (
         (ig_hbm, ig), (va_hbm, va), (og_hbm, og), (go_hbm, go), (taps_hbm, taps),
-        (entry_nat_hbm, entry_nat_in), (cos_hbm, cos), (sin_hbm, sin), (fwd_hbm, fwd_in),
-        (entry_hbm, entry_in), (inv_hbm, inv_in), (leave_hbm, leave_in),
-        (leave_nat_hbm, leave_nat_in), (gain_hbm, gain),
+        (entry_hbm, entry_in), (cos_hbm, cos), (sin_hbm, sin), (fwd_hbm, fwd_in),
+        (inv_hbm, inv_in), (leave_hbm, leave_in), (gain_hbm, gain),
     )
     loads = [pltpu.make_async_copy(src, dst, load_sem.at[i]) for i, (src, dst) in enumerate(pairs)]
     for load in loads[:4]:
@@ -116,6 +105,10 @@
     def near_peer(i):
         t = lax.rem(h + i, near)
         return t, (d, g * near + t)
+
+    def any_peer(i):
+        t = lax.rem(c + i, ctx)
+        return t, (d, t)
 
     barrier = pltpu.get_barrier_semaphore()
 
@@ -143,6 +136,13 @@
 
     for load in loads[4:]:
         load.start()
+
+    part = ctx // 2
+    by_channel[...] = selector(
+        4 * part, lambda r: (r % 4) // 2 * ctx + r // 4 * 2 + r % 2
+    )
+    by_piece[...] = selector(4 * part, lambda r: r % 4 * part + r // 4)
+    of_piece[...] = selector(4 * part, lambda r: r % part * 4 + r // part)
 
     def send_all(peer, count, src, dst, own, sem):
         def step(i, carry):
@@ -160,8 +160,8 @@
         lax.fori_loop(1, count, step, 0)
 
     def wait_blocks(dst, count, sems, i):
-        part = dst.at[pl.ds(0, count - 1)]
-        pltpu.make_async_copy(part, part, sems.at[i]).wait()
+        blocks = dst.at[pl.ds(0, count - 1)]
+        pltpu.make_async_copy(blocks, blocks, sems.at[i]).wait()
 
     def wait_one(ref, sem):
         pltpu.make_async_copy(ref, ref, sem).wait()
@@ -178,17 +178,54 @@
     for i in range(4):
         loads[i].wait()
     mixed, gmix = product(ig, va), product(go, og)
-    for i, tokens in enumerate((mixed, gmix)):
-        send1[i] = flip(tokens).reshape(far, 2 * near, block)
-        recv1[i, g] = send1[i, g]
+    for q in range(2):
+        lanes = slice(q * ctx, (q + 1) * ctx)
+        rows = dot_rows(by_channel[...], jnp.concatenate([mixed[:, lanes], gmix[:, lanes]], 1))
+        there_out[pl.ds(q * part, part)] = rows.astype(BF16).reshape(part, 4, block)
+    there_in[c] = there_out[c]
     near_sum[...] = jnp.sum(mixed.astype(F32) * gmix.astype(F32), axis=0, keepdims=True)
     near_recv[h] = near_sum[...]
     word[...] = jnp.zeros(word.shape, F32)
 
     pl.semaphore_wait(barrier, far + near - 2 + ahead)
-    for i in range(2):
-        send_all(far_peer, far, lambda t: send1.at[i, t], recv1.at[i], g, i)
-    send_all(near_peer, near, lambda t: near_sum, near_recv, h, 8)
+
+    def second(i, carry):
+        pl.semaphore_signal(ready, inc=1, device_id=near_peer(i)[1], device_id_type=MESH)
+        return carry
+
+    lax.fori_loop(1, near, second, 0)
+
+    def send_there(i, k):
+        t = lax.rem(g + i, far) * near + lax.rem(h + k, near)
+        pltpu.make_async_remote_copy(
+            src_ref=there_out.at[t],
+            dst_ref=there_in.at[c],
+            send_sem=send_sem.at[0],
+            recv_sem=recv_sem.at[0],
+            device_id=(d, t),
+            device_id_type=MESH,
+        ).start()
+
+    def far_step(i, carry):
+        send_there(i, 0)
+        return carry
+
+    def near_step(k, carry):
+        send_there(0, k)
+        return carry
+
+    def other_step(k, carry):
+        def step(i, inner):
+            send_there(i, k)
+            return inner
+
+        return lax.fori_loop(1, far, step, carry)
+
+    lax.fori_loop(1, far, far_step, 0)
+    lax.fori_loop(1, near, near_step, 0)
+    pl.semaphore_wait(ready, near - 1)
+    lax.fori_loop(1, near, other_step, 0)
+    send_all(near_peer, near, lambda t: near_sum, near_recv, h, 2)
     for t in others:
 
         @pl.when(order(t) < ahead)
@@ -228,49 +265,47 @@
         turned = jnp.concatenate([jnp.concatenate(real, 1), jnp.concatenate(imag, 1)], 0)
         return dot(table, turned).astype(BF16)
 
-    for i in range(4, 14):
+    for i in range(4, 12):
         loads[i].wait()
-    entry_nat[...] = entry_nat_in[...].astype(BF16)
+    entry[...] = entry_in[...].astype(BF16)
     fwd[...] = fwd_in[...].astype(BF16)
     for j in range(2):
         for a in range(ctx):
             taps_rows[j, pl.ds(a, 1)] = taps[pl.ds(j, 1), pl.ds(a * block, block)].astype(F32)
     both = jnp.concatenate([taps_rows[0], taps_rows[1]], 1).astype(BF16)
-    for j, spectrum in enumerate(forward(entry_nat[...], both)):
+    for j, spectrum in enumerate(forward(entry[...], both)):
         kern[j] = spectrum
-    entry[...] = entry_in[...].astype(BF16)
     inv[...] = inv_in[...].astype(BF16)
     leave[...] = leave_in[...].astype(BF16)
-    leave_nat[...] = leave_nat_in[...].astype(BF16)
-
-    for i in range(2):
-        wait_blocks(recv1.at[i], far, recv_sem, i)
-        rows = regroup(recv1[i].reshape(chans, block), far, 2 * near)
-        send2[i] = rows.reshape(near, 2, far, block)
-        recv2[i, h] = send2[i, h]
-        send_all(near_peer, near, lambda t: send2.at[i, t], recv2.at[i], h, 2 + i)
-
-    wait_blocks(near_recv, near, recv_sem, 8)
+
+    wait_blocks(near_recv, near, recv_sem, 2)
     far_sum[...] = total(near_recv, near)
     far_recv[g] = far_sum[...]
-    send_all(far_peer, far, lambda t: far_sum, far_recv, g, 9)
-
+    send_all(far_peer, far, lambda t: far_sum, far_recv, g, 3)
+
+    wait_blocks(there_in, ctx, recv_sem, 0)
+    halves = []
+    for q in range(2):
+        rows = there_in[pl.ds(q * part, part)].reshape(4 * part, block)
+        halves.append(dot(of_piece[...], rows).astype(BF16))
+    lines = [
+        jnp.concatenate([rows[i * part : (i + 1) * part] for rows in halves], 0) for i in range(4)
+    ]
     spectra = []
     for i in range(2):
-        wait_blocks(recv2.at[i], near, recv_sem, 2 + i)
-        both = jnp.concatenate([recv2[i, :, j].reshape(ctx, block) for j in range(2)], 1)
+        both = jnp.concatenate(lines[2 * i : 2 * i + 2], 1)
         spectra.append([(s[:, :block], s[:, block:]) for s in forward(entry[...], both)])
     sources, gradients = spectra
 
     specs = []
     for (ur, ui), (vr, vi) in zip(sources, gradients):
         specs.append(jnp.concatenate([ur * vr + ui * vi, ur * vi - ui * vr], 1).astype(BF16))
-    term = inverse(leave_nat[...], specs)
+    term = inverse(leave[...], specs)
     for j in range(2):
-        part = term[:, j * block : (j + 1) * block]
-        fsend[:, j] = part.reshape(n_dp, ctx // n_dp, block)
+        line = term[:, j * block : (j + 1) * block]
+        fsend[:, j] = line.reshape(n_dp, ctx // n_dp, block)
     frecv[d] = fsend[d]
-    wait_blocks(far_recv, far, recv_sem, 9)
+    wait_blocks(far_recv, far, recv_sem, 3)
     dp_sum[...] = total(far_recv, far)
     dp_recv[d] = dp_sum[...]
 
@@ -299,13 +334,16 @@
     for (ur, ui), (vr, vi), (kr, ki) in zip(sources, gradients, kernels):
         convs.append(jnp.concatenate([ur * kr - ui * ki, ur * ki + ui * kr], 1).astype(BF16))
         backs.append(jnp.concatenate([kr * vr + ki * vi, kr * vi - ki * vr], 1).astype(BF16))
-    for i, specs in enumerate((convs, backs)):
+    lines = []
+    for specs in (convs, backs):
         both = inverse(leave[...], specs)
-        for j in range(2):
-            part = both[:, j * block : (j + 1) * block]
-            send3[i, :, j] = part.reshape(near, far, block)
-        recv3[i, h] = send3[i, h]
-        send_all(near_peer, near, lambda t: send3.at[i, t], recv3.at[i], h, 4 + i)
+        lines += [both[:, :block], both[:, block:]]
+    for q in range(2):
+        rows = jnp.concatenate([x[q * part : (q + 1) * part] for x in lines], 0)
+        rows = dot(by_piece[...], rows).astype(BF16)
+        back_out[pl.ds(q * part, part)] = rows.reshape(part, 4, block)
+    back_in[c] = back_out[c]
+    send_all(any_peer, ctx, lambda t: back_out.at[t], back_in, c, 1)
 
     for t in others:
 
@@ -314,22 +352,20 @@
             wait_one(words.at[t], wrecv_sem.at[t])
             send_shares(t)
 
-    for i in range(2):
-        wait_blocks(recv3.at[i], near, recv_sem, 4 + i)
-        rows = regroup(recv3[i].reshape(chans, block), 2 * near, far)
-        send4[i] = rows.reshape(far, 2 * near, block)
-        recv4[i, g] = send4[i, g]
-        send_all(far_peer, far, lambda t: send4.at[i, t], recv4.at[i], g, 6 + i)
-
-    wait_blocks(recv4.at[0], far, recv_sem, 6)
-    conv = flip(recv4[0].reshape(chans, block)).astype(F32)
+    wait_blocks(back_in, ctx, recv_sem, 1)
+    eye = selector(block, lambda r: r)
+    convs, backs = [], []
+    for q in range(2):
+        rows = back_in[pl.ds(q * part, part)].reshape(4 * part, block)
+        rows = dot(dot_rows(eye, rows).astype(BF16), by_channel[...])
+        convs.append(rows[:, :ctx])
+        backs.append(rows[:, ctx:])
     gains = gain[...]
     gout[...] = (
-        go[...].astype(F32) * (conv + gains * product(ig, va).astype(F32))
+        go[...].astype(F32)
+        * (jnp.concatenate(convs, 1) + gains * product(ig, va).astype(F32))
     ).astype(BF16)
-    wait_blocks(recv4.at[1], far, recv_sem, 7)
-    back = flip(recv4[1].reshape(chans, block)).astype(F32)
-    grad_mixed = back + gains * product(go, og).astype(F32)
+    grad_mixed = jnp.concatenate(backs, 1) + gains * product(go, og).astype(F32)
     gin[...] = (grad_mixed * va[...].astype(F32)).astype(BF16)
     gval[...] = (grad_mixed * ig[...].astype(F32)).astype(BF16)
 
@@ -347,13 +383,10 @@
         wait_one(dp_recv.at[t], drecv_sem.at[t])
     skip_out[...] = total(dp_recv, n_dp) * scale
 
-    for i in range(2):
-        wait_blocks(recv1.at[i], far, send_sem, i)
-        wait_blocks(recv2.at[i], near, send_sem, 2 + i)
-        wait_blocks(recv3.at[i], near, send_sem, 4 + i)
-        wait_blocks(recv4.at[i], far, send_sem, 6 + i)
-    wait_blocks(near_recv, near, send_sem, 8)
-    wait_blocks(far_recv, far, send_sem, 9)
+    wait_blocks(there_in, ctx, send_sem, 0)
+    wait_blocks(back_in, ctx, send_sem, 1)
+    wait_blocks(near_recv, near, send_sem, 2)
+    wait_blocks(far_recv, far, send_sem, 3)
     for t in others:
         wait_one(fsend.at[t], fsend_sem.at[t])
         wait_one(dp_sum, dsend_sem.at[t])
@@ -377,8 +410,7 @@
     ctx = lax.axis_size("context")
     far, near = group_sizes(ctx)
     block, chans = input_gate.shape[1:]
-    rows = np.arange(ctx).reshape(far, near).T.reshape(-1)
-    tables = dft_tables(ctx, block, rows, 1.0 / (2 * ctx * block))
+    tables = dft_tables(ctx, block, 1.0 / (2 * ctx * block))
     gates = (input_gate[0], values[0], output_gate[0], grad_out[0], skip_gain.reshape(1, -1))
     operands = gates + (filter_taps,) + tables
     share = ctx // n_dp
@@ -395,18 +427,18 @@
         out_specs=tuple(pl.BlockSpec(memory_space=pltpu.VMEM) for _ in outs),
         scratch_shapes=[vmem(x.shape, x.dtype) for x in operands]
         + [vmem((2, ctx, block), F32)]
-        + [vmem(tables[i].shape, BF16) for i in (0, 3, 4, 5, 6, 7)]
-        + [vmem((2, far, 2 * near, block), BF16)] * 2
-        + [vmem((2, near, 2, far, block), BF16)] * 4
-        + [vmem((2, far, 2 * near, block), BF16)] * 2
+        + [vmem(tables[i].shape, BF16) for i in (0, 3, 4, 5)]
+        + [vmem((2 * ctx, 2 * ctx), BF16)] * 3
+        + [vmem((ctx, 4, block), BF16)] * 4
         + [vmem((1, chans), F32), vmem((near, 1, chans), F32)]
         + [vmem((1, chans), F32), vmem((far, 1, chans), F32)]
         + [vmem((n_dp, 2, share, block), BF16)] * 2
         + [vmem((1, chans), F32), vmem((n_dp, 1, chans), F32)]
         + [vmem((1, 128), F32), vmem((n_dp, 1, 128), F32)]
         + [vmem((2, 2 * ctx, 2 * block), F32)]
-        + [dma((len(operands),)), dma((10,)), dma((10,))]
-        + [dma((n_dp,))] * 6,
+        + [dma((len(operands),)), dma((4,)), dma((4,))]
+        + [dma((n_dp,))] * 6
+        + [pltpu.SemaphoreType.REGULAR],
         compiler_params=pltpu.CompilerParams(
             collective_id=0, has_side_effects=True, vmem_limit_bytes=32 * 1024 * 1024
         ),

time: 35.2 us -> 34.1 us (0.969)
  Pallas kernels: 34.4 us -> 32.9 us
    pallas_call x1, Pallas kernels: 33.6 us -> 32.2 us  [per_device(): pl.pallas_call(functools.partial(mixer_kernel, (n_dp, far, near, chans, b...]
where the time goes in v6:
time: 34.1 us; the launch traced here: 33.6 us
  Pallas kernels  32.9 us (96%)
  between operations  0.64 us (2%)
    pallas_call x1, Pallas kernels, per_device(): pl.pallas_call(functools.partial(mixer_kernel, (n_dp, far, near, chans, b...  32.2 us
    pallas_call x1, Pallas kernels, per_device(): pl.pallas_call(copy_kernel, out_shape=outs, in_specs=[pl.BlockSpec(memory...  0.73 us

profile of v6, /device:TPU:1, one launch (start us, length us, event | category | flops | bytes accessed | tf_op | source)
XLA Modules:
  0.0 33.6 jit_solution(10417684031628957942)
XLA Ops:
  0.6 32.2 %mixer.1 = (bf16[128,256]{1,0:T(8,128)(2,1)S(1)}, bf16[128,256]{1,0:T(8,128)(2,1)S(1)}, bf16[128,256]{1,0:T(8,128)(2,1)S(1)}, f32[2,4096]{1,0:T(2,128)S(1)}, f32[1,256]{1,0:T(1,128)S(1)}) custom-call(bf16[128,256]{1,0:T(8,128)(2,1)} %bitcast.9, bf16[128,256]{1,0:T(8,128)(2,1)} %bitcast.10, bf16[128,256]{1,0:T(8,128)(2,1)} %bitcast.11, ...), custom_call_target="tpu_custom_call" | custom-call | tf_op jit(solution)/shard_map/mixer/pallas_call | solution.py:423
  32.9 0.7 %results.1 = (bf16[128,256]{1,0:T(8,128)(2,1)}, bf16[128,256]{1,0:T(8,128)(2,1)}, bf16[128,256]{1,0:T(8,128)(2,1)}, f32[2,4096]{1,0:T(2,128)}, f32[1,256]{1,0:T(1,128)}) custom-call(bf16[128,256]{1,0:T(8,128)(2,1)S(1)} %get-tuple-element.15.refs_0_, bf16[128,256]{1,0:T(8,128)(2,1)S(1)} %get-tuple-element.16.refs_1_, ...), custom_call_target="tpu_custom_call" | custom-call | tf_op jit(solution)/shard_map/results/pallas_call | solution.py:447

commit v7 on v6

--- a/solution.py
+++ b/solution.py
@@ -95,8 +95,6 @@
         (inv_hbm, inv_in), (leave_hbm, leave_in), (gain_hbm, gain),
     )
     loads = [pltpu.make_async_copy(src, dst, load_sem.at[i]) for i, (src, dst) in enumerate(pairs)]
-    for load in loads[:4]:
-        load.start()
 
     def far_peer(i):
         t = lax.rem(g + i, far)
@@ -106,18 +104,39 @@
         t = lax.rem(h + i, near)
         return t, (d, g * near + t)
 
-    def any_peer(i):
-        t = lax.rem(c + i, ctx)
-        return t, (d, t)
+    n_y = int(math.isqrt(far))
+    n_z, n_x = far // n_y, near // 2
+    z, y, x, core = g // n_y, lax.rem(g, n_y), h // 2, lax.rem(h, 2)
+    turns_y = sorted(range(n_y), key=lambda v: -min(v, n_y - v))
+    turns_x = sorted(range(n_x), key=lambda v: -min(v, n_x - v))
+    spots = [(i, j) for i in turns_x for j in (1, 0)]
+
+    def around(act, spots):
+        def step(s, carry):
+            there = s + (1 - z // (n_z // 2)) * (n_z - 1 - 2 * s)
+            for turn in turns_y:
+                row = there * n_y + lax.rem(y + turn, n_y)
+
+                def go():
+                    for i, j in spots:
+                        act(row * near + lax.rem(x + i, n_x) * 2 + lax.rem(core + j, 2))
+
+                if turn == 0:
+                    pl.when(row != g)(go)
+                else:
+                    go()
+            return carry
+
+        lax.fori_loop(0, n_z, step, 0)
+
+    def within(act):
+        for i, j in spots[:-1]:
+            act(g * near + lax.rem(x + i, n_x) * 2 + lax.rem(core + j, 2))
 
     barrier = pltpu.get_barrier_semaphore()
 
-    def greet(peer):
-        def step(i, carry):
-            pl.semaphore_signal(barrier, inc=1, device_id=peer(i)[1], device_id_type=MESH)
-            return carry
-
-        return step
+    def greet(t):
+        pl.semaphore_signal(barrier, inc=1, device_id=(d, t), device_id_type=MESH)
 
     half = n_dp // 2
 
@@ -126,15 +145,15 @@
 
     ahead = order(d)
     others = [lax.rem(d + n_dp - i, n_dp) for i in (2, 1, 3)[: n_dp - 1]] if n_dp > 2 else [1 - d]
-    lax.fori_loop(1, far, greet(far_peer), 0)
-    lax.fori_loop(1, near, greet(near_peer), 0)
+    around(greet, spots[-1:])
+    within(greet)
     for t in others:
 
         @pl.when(order(t) > ahead)
         def _():
             pl.semaphore_signal(barrier, inc=1, device_id=(t, c), device_id_type=MESH)
 
-    for load in loads[4:]:
+    for load in loads:
         load.start()
 
     part = ctx // 2
@@ -189,43 +208,34 @@
 
     pl.semaphore_wait(barrier, far + near - 2 + ahead)
 
-    def second(i, carry):
-        pl.semaphore_signal(ready, inc=1, device_id=near_peer(i)[1], device_id_type=MESH)
-        return carry
-
-    lax.fori_loop(1, near, second, 0)
-
-    def send_there(i, k):
-        t = lax.rem(g + i, far) * near + lax.rem(h + k, near)
-        pltpu.make_async_remote_copy(
-            src_ref=there_out.at[t],
-            dst_ref=there_in.at[c],
-            send_sem=send_sem.at[0],
-            recv_sem=recv_sem.at[0],
-            device_id=(d, t),
-            device_id_type=MESH,
-        ).start()
-
-    def far_step(i, carry):
-        send_there(i, 0)
-        return carry
-
-    def near_step(k, carry):
-        send_there(0, k)
-        return carry
-
-    def other_step(k, carry):
-        def step(i, inner):
-            send_there(i, k)
-            return inner
-
-        return lax.fori_loop(1, far, step, carry)
-
-    lax.fori_loop(1, far, far_step, 0)
-    lax.fori_loop(1, near, near_step, 0)
+    def second(t):
+        pl.semaphore_signal(ready, inc=1, device_id=(d, t), device_id_type=MESH)
+
+    within(second)
+
+    def send_piece(src, dst, sem):
+        def send(t):
+            pltpu.make_async_remote_copy(
+                src_ref=src.at[t],
+                dst_ref=dst.at[c],
+                send_sem=send_sem.at[sem],
+                recv_sem=recv_sem.at[sem],
+                device_id=(d, t),
+                device_id_type=MESH,
+            ).start()
+
+        return send
+
+    send_there = send_piece(there_out, there_in, 0)
+    around(send_there, spots[-1:])
+    send_all(near_peer, near, lambda t: near_sum, near_recv, h, 2)
+    within(send_there)
     pl.semaphore_wait(ready, near - 1)
-    lax.fori_loop(1, near, other_step, 0)
-    send_all(near_peer, near, lambda t: near_sum, near_recv, h, 2)
+    around(send_there, spots[:-1])
+    wait_blocks(near_recv, near, recv_sem, 2)
+    far_sum[...] = total(near_recv, near)
+    far_recv[g] = far_sum[...]
+    send_all(far_peer, far, lambda t: far_sum, far_recv, g, 3)
     for t in others:
 
         @pl.when(order(t) < ahead)
@@ -278,11 +288,6 @@
     inv[...] = inv_in[...].astype(BF16)
     leave[...] = leave_in[...].astype(BF16)
 
-    wait_blocks(near_recv, near, recv_sem, 2)
-    far_sum[...] = total(near_recv, near)
-    far_recv[g] = far_sum[...]
-    send_all(far_peer, far, lambda t: far_sum, far_recv, g, 3)
-
     wait_blocks(there_in, ctx, recv_sem, 0)
     halves = []
     for q in range(2):
@@ -343,7 +348,9 @@
         rows = dot(by_piece[...], rows).astype(BF16)
         back_out[pl.ds(q * part, part)] = rows.reshape(part, 4, block)
     back_in[c] = back_out[c]
-    send_all(any_peer, ctx, lambda t: back_out.at[t], back_in, c, 1)
+    send_back = send_piece(back_out, back_in, 1)
+    around(send_back, spots)
+    within(send_back)
 
     for t in others:
 

time: 34.1 us -> 33.1 us (0.971)
  the two profiles are of different devices: /device:TPU:1 before, /device:TPU:32 now
where the time goes in v7:
time: 33.1 us; the launch traced here: 32.9 us
  Pallas kernels  32.3 us (98%)
  between operations  0.64 us (2%)
    pallas_call x1, Pallas kernels, per_device(): pl.pallas_call(functools.partial(mixer_kernel, (n_dp, far, near, chans, b...  31.6 us
    pallas_call x1, Pallas kernels, per_device(): pl.pallas_call(copy_kernel, out_shape=outs, in_specs=[pl.BlockSpec(memory...  0.73 us

profile of v7, /device:TPU:32, one launch (start us, length us, event | category | flops | bytes accessed | tf_op | source)
XLA Modules:
  0.0 32.9 jit_solution(3363665413918927739)
XLA Ops:
  0.6 31.6 %mixer.1 = (bf16[128,256]{1,0:T(8,128)(2,1)S(1)}, bf16[128,256]{1,0:T(8,128)(2,1)S(1)}, bf16[128,256]{1,0:T(8,128)(2,1)S(1)}, f32[2,4096]{1,0:T(2,128)S(1)}, f32[1,256]{1,0:T(1,128)S(1)}) custom-call(bf16[128,256]{1,0:T(8,128)(2,1)} %bitcast.9, bf16[128,256]{1,0:T(8,128)(2,1)} %bitcast.10, bf16[128,256]{1,0:T(8,128)(2,1)} %bitcast.11, ...), custom_call_target="tpu_custom_call" | custom-call | tf_op jit(solution)/shard_map/mixer/pallas_call | solution.py:430
  32.2 0.7 %results.1 = (bf16[128,256]{1,0:T(8,128)(2,1)}, bf16[128,256]{1,0:T(8,128)(2,1)}, bf16[128,256]{1,0:T(8,128)(2,1)}, f32[2,4096]{1,0:T(2,128)}, f32[1,256]{1,0:T(1,128)}) custom-call(bf16[128,256]{1,0:T(8,128)(2,1)S(1)} %get-tuple-element.15.refs_0_, bf16[128,256]{1,0:T(8,128)(2,1)S(1)} %get-tuple-element.16.refs_1_, ...), custom_call_target="tpu_custom_call" | custom-call | tf_op jit(solution)/shard_map/results/pallas_call | solution.py:454

commit v8 on v7

--- a/solution.py
+++ b/solution.py
@@ -79,7 +79,7 @@
     there_out, there_in, back_out, back_in,
     near_sum, near_recv, far_sum, far_recv, fsend, frecv, dp_sum, dp_recv, word, words, kern,
     load_sem, send_sem, recv_sem, fsend_sem, frecv_sem, dsend_sem, drecv_sem,
-    wsend_sem, wrecv_sem, ready,
+    wsend_sem, wrecv_sem,
 ):
     n_dp, far, near, chans, block = sizes
     ctx = far * near
@@ -145,7 +145,9 @@
 
     ahead = order(d)
     others = [lax.rem(d + n_dp - i, n_dp) for i in (2, 1, 3)[: n_dp - 1]] if n_dp > 2 else [1 - d]
-    around(greet, spots[-1:])
+    for load in loads[:4]:
+        load.start()
+    around(greet, spots)
     within(greet)
     for t in others:
 
@@ -153,7 +155,7 @@
         def _():
             pl.semaphore_signal(barrier, inc=1, device_id=(t, c), device_id_type=MESH)
 
-    for load in loads:
+    for load in loads[4:]:
         load.start()
 
     part = ctx // 2
@@ -206,12 +208,7 @@
     near_recv[h] = near_sum[...]
     word[...] = jnp.zeros(word.shape, F32)
 
-    pl.semaphore_wait(barrier, far + near - 2 + ahead)
-
-    def second(t):
-        pl.semaphore_signal(ready, inc=1, device_id=(d, t), device_id_type=MESH)
-
-    within(second)
+    pl.semaphore_wait(barrier, ctx - 1 + ahead)
 
     def send_piece(src, dst, sem):
         def send(t):
@@ -227,11 +224,9 @@
         return send
 
     send_there = send_piece(there_out, there_in, 0)
-    around(send_there, spots[-1:])
     send_all(near_peer, near, lambda t: near_sum, near_recv, h, 2)
+    around(send_there, spots)
     within(send_there)
-    pl.semaphore_wait(ready, near - 1)
-    around(send_there, spots[:-1])
     wait_blocks(near_recv, near, recv_sem, 2)
     far_sum[...] = total(near_recv, near)
     far_recv[g] = far_sum[...]
@@ -309,30 +304,29 @@
     for j in range(2):
         line = term[:, j * block : (j + 1) * block]
         fsend[:, j] = line.reshape(n_dp, ctx // n_dp, block)
+
+    def send_share(src, dst, out, come, t):
+        pltpu.make_async_remote_copy(
+            src_ref=src,
+            dst_ref=dst.at[d],
+            send_sem=out.at[t],
+            recv_sem=come.at[d],
+            device_id=(t, c),
+            device_id_type=MESH,
+        ).start()
+
+    def send_filter(t):
+        send_share(fsend.at[t], frecv, fsend_sem, frecv_sem, t)
+
+    def send_sum(t):
+        send_share(dp_sum, dp_recv, dsend_sem, drecv_sem, t)
+
+    pl.when(ahead > 0)(functools.partial(send_filter, 0))
     frecv[d] = fsend[d]
     wait_blocks(far_recv, far, recv_sem, 3)
     dp_sum[...] = total(far_recv, far)
+    pl.when(ahead > 0)(functools.partial(send_sum, 0))
     dp_recv[d] = dp_sum[...]
-
-    def send_shares(t):
-        for src, dst, out, come in (
-            (fsend.at[t], frecv.at[d], fsend_sem.at[t], frecv_sem.at[d]),
-            (dp_sum, dp_recv.at[d], dsend_sem.at[t], drecv_sem.at[d]),
-        ):
-            pltpu.make_async_remote_copy(
-                src_ref=src,
-                dst_ref=dst,
-                send_sem=out,
-                recv_sem=come,
-                device_id=(t, c),
-                device_id_type=MESH,
-            ).start()
-
-    for t in others:
-
-        @pl.when(order(t) < ahead)
-        def _():
-            send_shares(t)
 
     kernels = [(kern[j][:, :block], kern[j][:, block:]) for j in range(2)]
     convs, backs = [], []
@@ -348,16 +342,26 @@
         rows = dot(by_piece[...], rows).astype(BF16)
         back_out[pl.ds(q * part, part)] = rows.reshape(part, 4, block)
     back_in[c] = back_out[c]
+
+    @pl.when(ahead > 1)
+    def _():
+        send_filter(1)
+        send_sum(1)
+
     send_back = send_piece(back_out, back_in, 1)
     around(send_back, spots)
     within(send_back)
 
-    for t in others:
+    for t in others[::-1]:
 
         @pl.when(order(t) > ahead)
         def _():
             wait_one(words.at[t], wrecv_sem.at[t])
-            send_shares(t)
+
+        @pl.when((t > 1) | ((t == 1) & (ahead <= 1)))
+        def _():
+            send_filter(t)
+            send_sum(t)
 
     wait_blocks(back_in, ctx, recv_sem, 1)
     eye = selector(block, lambda r: r)
@@ -444,8 +448,7 @@
         + [vmem((1, 128), F32), vmem((n_dp, 1, 128), F32)]
         + [vmem((2, 2 * ctx, 2 * block), F32)]
         + [dma((len(operands),)), dma((4,)), dma((4,))]
-        + [dma((n_dp,))] * 6
-        + [pltpu.SemaphoreType.REGULAR],
+        + [dma((n_dp,))] * 6,
         compiler_params=pltpu.CompilerParams(
             collective_id=0, has_side_effects=True, vmem_limit_bytes=32 * 1024 * 1024
         ),

time: 33.1 us -> 31.6 us (0.955)
  the two profiles are of different devices: /device:TPU:32 before, /device:TPU:1 now
where the time goes in v8:
time: 31.6 us; the launch traced here: 31.5 us
  Pallas kernels  30.9 us (98%)
  between operations  0.64 us (2%)
    pallas_call x1, Pallas kernels, per_device(): pl.pallas_call(functools.partial(mixer_kernel, (n_dp, far, near, chans, b...  30.1 us
    pallas_call x1, Pallas kernels, per_device(): pl.pallas_call(copy_kernel, out_shape=outs, in_specs=[pl.BlockSpec(memory...  0.73 us

profile of v8, /device:TPU:1, one launch (start us, length us, event | category | flops | bytes accessed | tf_op | source)
XLA Modules:
  0.0 31.5 jit_solution(17378204452293006278)
XLA Ops:
  0.6 30.1 %mixer.1 = (bf16[128,256]{1,0:T(8,128)(2,1)S(1)}, bf16[128,256]{1,0:T(8,128)(2,1)S(1)}, bf16[128,256]{1,0:T(8,128)(2,1)S(1)}, f32[2,4096]{1,0:T(2,128)S(1)}, f32[1,256]{1,0:T(1,128)S(1)}) custom-call(bf16[128,256]{1,0:T(8,128)(2,1)} %bitcast.9, bf16[128,256]{1,0:T(8,128)(2,1)} %bitcast.10, bf16[128,256]{1,0:T(8,128)(2,1)} %bitcast.11, ...), custom_call_target="tpu_custom_call" | custom-call | tf_op jit(solution)/shard_map/mixer/pallas_call | solution.py:434
  30.8 0.7 %results.1 = (bf16[128,256]{1,0:T(8,128)(2,1)}, bf16[128,256]{1,0:T(8,128)(2,1)}, bf16[128,256]{1,0:T(8,128)(2,1)}, f32[2,4096]{1,0:T(2,128)}, f32[1,256]{1,0:T(1,128)}) custom-call(bf16[128,256]{1,0:T(8,128)(2,1)S(1)} %get-tuple-element.15.refs_0_, bf16[128,256]{1,0:T(8,128)(2,1)S(1)} %get-tuple-element.16.refs_1_, ...), custom_call_target="tpu_custom_call" | custom-call | tf_op jit(solution)/shard_map/results/pallas_call | solution.py:457

commit v9 on v8

--- a/solution.py
+++ b/solution.py
@@ -227,10 +227,6 @@
     send_all(near_peer, near, lambda t: near_sum, near_recv, h, 2)
     around(send_there, spots)
     within(send_there)
-    wait_blocks(near_recv, near, recv_sem, 2)
-    far_sum[...] = total(near_recv, near)
-    far_recv[g] = far_sum[...]
-    send_all(far_peer, far, lambda t: far_sum, far_recv, g, 3)
     for t in others:
 
         @pl.when(order(t) < ahead)
@@ -243,6 +239,11 @@
                 device_id=(t, c),
                 device_id_type=MESH,
             ).start()
+
+    wait_blocks(near_recv, near, recv_sem, 2)
+    far_sum[...] = total(near_recv, near)
+    far_recv[g] = far_sum[...]
+    send_all(far_peer, far, lambda t: far_sum, far_recv, g, 3)
 
     def forward(table, x):
         section = dot(table, x)

time: 31.6 us -> 31.7 us (level)
  no operation moved by 1% of the time
where the time goes in v9:
time: 31.7 us; the launch traced here: 31.5 us
  Pallas kernels  30.9 us (97%)
  between operations  0.64 us (2%)
    pallas_call x1, Pallas kernels, per_device(): pl.pallas_call(functools.partial(mixer_kernel, (n_dp, far, near, chans, b...  30.1 us
    pallas_call x1, Pallas kernels, per_device(): pl.pallas_call(copy_kernel, out_shape=outs, in_specs=[pl.BlockSpec(memory...  0.73 us

profile of v9, /device:TPU:1, one launch (start us, length us, event | category | flops | bytes accessed | tf_op | source)
XLA Modules:
  0.0 31.5 jit_solution(2836823351539207519)
XLA Ops:
  0.6 30.1 %mixer.1 = (bf16[128,256]{1,0:T(8,128)(2,1)S(1)}, bf16[128,256]{1,0:T(8,128)(2,1)S(1)}, bf16[128,256]{1,0:T(8,128)(2,1)S(1)}, f32[2,4096]{1,0:T(2,128)S(1)}, f32[1,256]{1,0:T(1,128)S(1)}) custom-call(bf16[128,256]{1,0:T(8,128)(2,1)} %bitcast.9, bf16[128,256]{1,0:T(8,128)(2,1)} %bitcast.10, bf16[128,256]{1,0:T(8,128)(2,1)} %bitcast.11, ...), custom_call_target="tpu_custom_call" | custom-call | tf_op jit(solution)/shard_map/mixer/pallas_call | solution.py:435
  30.8 0.7 %results.1 = (bf16[128,256]{1,0:T(8,128)(2,1)}, bf16[128,256]{1,0:T(8,128)(2,1)}, bf16[128,256]{1,0:T(8,128)(2,1)}, f32[2,4096]{1,0:T(2,128)}, f32[1,256]{1,0:T(1,128)}) custom-call(bf16[128,256]{1,0:T(8,128)(2,1)S(1)} %get-tuple-element.15.refs_0_, bf16[128,256]{1,0:T(8,128)(2,1)S(1)} %get-tuple-element.16.refs_1_, ...), custom_call_target="tpu_custom_call" | custom-call | tf_op jit(solution)/shard_map/results/pallas_call | solution.py:458
